TPU v7x, 32 devices: a whole 2x2x4 slice. The times are simulated.
32 devices in a mesh: space: 4 (over y, x), tm: 8 (over z, core).
Axes of the slice: x: 2, y: 2, z: 4, core: 2. Of those that a mesh axis runs over, the one named last changes fastest.
Arguments:
- initial_guess: float32 [4, 64, 32, 4, 128], P(None, 'tm', 'space'), may hold values from -6 to 6
- forcing: float32 [4, 64, 32, 4, 128], P(None, 'tm', 'space'), may hold values from -6 to 6
- visc_table: float32 [8], replicated, may hold values from 0.05 to 0.5
- visc_class: int32 [32, 4, 128], P('space'), may hold values from 0 to 7
- inverse_bank: bfloat16 [4, 32, 32], replicated, may hold values from -0.125 to 0.125
- patch_kind: int32 [16, 2, 64], P('space'), may hold values from 0 to 3
Outputs:
- smoothed: float32 [4, 64, 32, 4, 128], P(None, 'tm', 'space')
- coarse: float32 [4, 2, 16384], P(None, None, ('space', 'tm'))
All inputs are finite; a program needn't handle non-finite values.
Results may differ from a plain program's by a relative error of at most 0.00096.
Values sent between devices are 32-bit elements; how exact they have to be, the bound alone decides.
No kernel may reach another device: no remote copies, remote signals or barrier semaphores. Data moves between devices by JAX's collectives and lax.ppermute only.
A program may use at most 64 MiB of HBM per device.

v0:
```python
import jax
import jax.numpy as jnp
from jax import lax
from jax.sharding import PartitionSpec as P

SWEEPS = 2
LEVELS = 5


damping = 0.8
mass_weight = 1.0
stabilize = 0.1


def extended_2(shard, sides, width):
    for axis, dim in sides:
        size, length = (lax.axis_size(axis), shard.shape[dim])
        up = [(i, (i + 1) % size) for i in range(size - 1)]
        down = [(j, i) for i, j in up]
        last = lax.slice_in_dim(shard, length - width, length, axis=dim)
        leading = lax.slice_in_dim(shard, 0, width, axis=dim)
        before = lax.ppermute(last, axis, up)
        after = lax.ppermute(leading, axis, down)
        shard = jnp.concatenate([before, shard, after], axis=dim)
    return shard


def passed_along(shard, axis, by):
    length = lax.axis_size(axis)
    pairs = [(i, i + by) for i in range(length) if 0 <= i + by < length]
    return lax.ppermute(shard, axis, pairs)


def neighbour(array, offset):
    size_x = array.shape[-3] - 2
    size_y = array.shape[-2] - 2
    size_z = array.shape[-1] - 2
    return array[
        ...,
        1 + offset[0] : 1 + offset[0] + size_x,
        1 + offset[1] : 1 + offset[1] + size_y,
        1 + offset[2] : 1 + offset[2] + size_z,
    ]


def operate(padded, earlier, visc_pad):
    extended = jnp.pad(padded, ((0, 0), (0, 0), (0, 0), (1, 1), (1, 1)))
    viscous = jnp.pad(visc_pad, ((0, 0), (1, 1), (1, 1)))
    centre = (0, 0, 0)
    centre_visc = neighbour(viscous, centre)
    velocity = neighbour(extended[:3], centre)
    pressure = neighbour(extended[3], centre)
    units = ((1, 0, 0), (0, 1, 0), (0, 0, 1))
    diffusion = jnp.zeros_like(velocity)
    pressure_sum = jnp.zeros_like(pressure)
    gradient = []
    divergence = jnp.zeros_like(pressure)
    for number in range(3):
        unit = units[number]
        minus = (-unit[0], -unit[1], -unit[2])
        for offset in (unit, minus):
            kappa = 0.5 * (centre_visc + neighbour(viscous, offset))
            diffusion = diffusion + kappa * (velocity - neighbour(extended[:3], offset))
            pressure_sum = pressure_sum + neighbour(extended[3], offset)
        gradient.append(0.5 * (neighbour(extended[3], unit) - neighbour(extended[3], minus)))
        divergence = divergence + 0.5 * (
            neighbour(extended[number], unit) - neighbour(extended[number], minus)
        )
    previous = jnp.concatenate([earlier[:, None], velocity[:, :-1]], axis=1)
    momentum = mass_weight * (velocity - previous) + diffusion + jnp.stack(gradient)
    continuity = stabilize * (6.0 * pressure - pressure_sum) - divergence
    return jnp.concatenate([momentum, continuity[None]], axis=0)


def lookup(classes, table):
    labels = jnp.arange(table.shape[0], dtype=jnp.int32).reshape(-1, 1, 1, 1)
    return jnp.sum(jnp.where(classes[None] == labels, table.reshape(-1, 1, 1, 1), 0.0), axis=0)


def vanka_patches(resid, inverse_bank, patch_kind):
    kinds_count = inverse_bank.shape[0]
    comps, steps, size_x, size_y, size_z = resid.shape
    pairs_x = size_x // 2
    quads_y = size_y // 4
    half_z = size_z // 2
    side_x = jnp.arange(2, dtype=jnp.int32).reshape(2, 1, 1)
    row_y = jnp.arange(4, dtype=jnp.int32).reshape(1, 4, 1)
    cell_z = jnp.arange(size_z, dtype=jnp.int32).reshape(1, 1, size_z)
    parity = 4 * side_x + 2 * (row_y % 2) + cell_z % 2
    column = parity * size_z + row_y // 2 * half_z + cell_z // 2
    targets = jnp.arange(8 * size_z, dtype=jnp.int32)
    permuter = (column[..., None] == targets).astype(jnp.bfloat16)
    blocks = resid.astype(jnp.bfloat16).reshape(comps, steps, pairs_x, 2, quads_y, 4, size_z)
    grouped = lax.dot_general(
        blocks, permuter, (((3, 5, 6), (0, 1, 2)), ((), ())), preferred_element_type=jnp.float32
    )
    grouped = grouped.astype(jnp.bfloat16).reshape(comps, steps, pairs_x, quads_y, 8, size_z)
    bank_flat = inverse_bank.reshape(kinds_count * 8 * comps, comps, 8)
    products = lax.dot_general(
        bank_flat, grouped, (((1, 2), (0, 4)), ((), ())), preferred_element_type=jnp.float32
    )
    products = products.reshape(kinds_count, comps, 8, steps, pairs_x, quads_y, size_z)
    kinds_flat = patch_kind.reshape(pairs_x, quads_y, size_z)
    labels = jnp.arange(kinds_count, dtype=jnp.int32).reshape(-1, 1, 1, 1, 1, 1, 1)
    chosen = jnp.sum(jnp.where(kinds_flat[None, None, None, None] == labels, products, 0.0), axis=0)
    scaled = damping * chosen
    back_table = permuter.astype(jnp.float32).reshape(2, 4, size_z, 8, size_z)
    placed = lax.dot_general(
        scaled,
        back_table,
        (((1, 5), (3, 4)), ((), ())),
        precision=lax.Precision.HIGHEST,
        preferred_element_type=jnp.float32,
    )
    placed = placed.transpose(0, 1, 2, 4, 3, 5, 6)
    return placed.reshape(comps, steps, size_x, size_y, size_z)


def coarsen(level_now, before_step):
    even_steps = level_now[:, 0::2]
    odd_steps = level_now[:, 1::2]
    shifted = jnp.concatenate([before_step[:, None], odd_steps[:, :-1]], axis=1)
    return 0.25 * shifted + 0.5 * even_steps + 0.25 * odd_steps


def per_device(initial_guess, forcing, visc_table, visc_class, inverse_bank, patch_kind):
    viscosity = lookup(visc_class, visc_table)
    visc_pad = extended_2(viscosity, (("space", 0),), 1)

    def residual_of(iterate):
        padded = extended_2(iterate, (("space", 2),), 1)
        earlier = passed_along(iterate[:3, -1], "tm", 1)
        return forcing - operate(padded, earlier, visc_pad)

    iterate = initial_guess
    for sweep_index in range(SWEEPS):
        iterate = iterate + vanka_patches(residual_of(iterate), inverse_bank, patch_kind)
    final = residual_of(iterate)
    flattened = final.reshape(final.shape[0], final.shape[1], -1)
    result = lax.all_to_all(flattened, "tm", split_axis=2, concat_axis=1, tiled=True)
    for level_index in range(LEVELS):
        result = coarsen(result, jnp.zeros_like(result[:, 0]))
    return (iterate, result)


def solution(mesh):
    return jax.shard_map(
        per_device,
        mesh=mesh,
        in_specs=(
            P(None, "tm", "space", None, None),
            P(None, "tm", "space", None, None),
            P(),
            P("space", None, None),
            P(),
            P("space", None, None),
        ),
        out_specs=(P(None, "tm", "space", None, None), P(None, None, ("space", "tm"))),
        check_vma=False,
    )
```

profile of v0, /device:TPU:0, one launch (start us, length us, event | category | flops | bytes accessed | tf_op | source)
XLA Modules:
  0.0 123.3 jit_solution(15605580217237756161)
XLA Ops:
  0.6 0.9 fusion.133
  1.5 1.3 %collective-permute-start.2 = (f32[4,8,1,4,128]{4,3,2,1,0:T(4,128)S(1)}, f32[4,8,1,4,128]{4,3,2,1,0:T(4,128)S(1)}, u32[]{:S(2)}, u32[]{:S(2)}) collective-permute-start(f32[4,8,1,4,128]{4,3,2,1,0:T(4,128)S(1)} %get-tuple-element.31), channel_id=1, source_target_pairs={{8,0},{16,8},{24,16},{9,1},{17,9},{25,17},{10,2},{18,10},{26,18},{... | collective-permute-start | bytes 196616 | tf_op jit(solution)/shard_map/ppermute | solution.py:23
  2.8 5.5 %collective-permute-start.4 = (f32[4,8,1,4,128]{4,3,2,1,0:T(4,128)S(1)}, f32[4,8,1,4,128]{4,3,2,1,0:T(4,128)S(1)}, u32[]{:S(2)}, u32[]{:S(2)}) collective-permute-start(f32[4,8,1,4,128]{4,3,2,1,0:T(4,128)S(1)} %get-tuple-element.30), channel_id=1, source_target_pairs={{0,8},{8,16},{16,24},{1,9},{9,17},{17,25},{2,10},{10,18},{18,26},{... | collective-permute-start | bytes 196616 | tf_op jit(solution)/shard_map/ppermute | solution.py:22
  8.3 0.7 copy.25
  9.0 0.7 select_reduce_fusion
  9.8 1.3 %collective-permute-start.1 = (f32[1,4,128]{2,0,1:T(1,128)S(1)}, f32[1,4,128]{2,0,1:T(1,128)S(1)}, u32[]{:S(2)}, u32[]{:S(2)}) collective-permute-start(f32[1,4,128]{2,0,1:T(1,128)S(1)} %get-tuple-element.39), channel_id=1, source_target_pairs={{8,0},{16,8},{24,16},{9,1},{17,9},{25,17},{10,2},{18,10},{26,18},{... | collective-permute-start | bytes 6152 | tf_op jit(solution)/shard_map/ppermute | solution.py:23
  11.1 5.4 %collective-permute-start.3 = (f32[1,4,128]{2,0,1:T(1,128)S(1)}, f32[1,4,128]{2,0,1:T(1,128)S(1)}, u32[]{:S(2)}, u32[]{:S(2)}) collective-permute-start(f32[1,4,128]{2,0,1:T(1,128)S(1)} %get-tuple-element.38), channel_id=1, source_target_pairs={{0,8},{8,16},{16,24},{1,9},{9,17},{17,25},{2,10},{10,18},{18,26},{... | collective-permute-start | bytes 6152 | tf_op jit(solution)/shard_map/ppermute | solution.py:22
  16.5 0.8 slice_bitcast_fusion.14
  17.3 1.3 %collective-permute-start = (f32[3,8,4,128]{3,2,1,0:T(4,128)S(1)}, f32[3,8,4,128]{3,2,1,0:T(4,128)S(1)}, u32[]{:S(2)}, u32[]{:S(2)}) collective-permute-start(f32[3,8,4,128]{3,2,1,0:T(4,128)S(1)} %slice_bitcast_fusion.14), channel_id=1, source_target_pairs={{0,1},{1,2},{2,3},{3,4},{4,5},{5,6},{6,7},{8,9},{9,10},{10,11},{11... | collective-permute-start | bytes 147464 | tf_op jit(solution)/shard_map/ppermute | solution.py:31
  18.7 0.8 eq.95
  19.5 0.1 broadcast_add_fusion
  19.5 0.1 add_add_fusion
  19.6 1.0 slice.472
  20.6 0.9 dot_general.25
  21.5 0.0 collective-permute-done.1
  21.5 0.1 select_maximum_fusion.6
  21.6 0.1 fusion.124
  21.8 0.0 collective-permute-done.2
  21.8 0.0 collective-permute-done.4
  21.8 1.8 %select_maximum_fusion.4 = f32[4,8,10,6,130]{4,3,2,1,0:T(8,128)S(1)} fusion(f32[4,8,1,4,128]{4,3,2,1,0:T(4,128)S(1)} %collective-permute-done.2, f32[4,8,8,4,128]{4,3,2,1,0:T(4,128)} %param.6, f32[4,8,1,4,128]{4,3,2,1,0:T(4,128)S(1)} %collective-permute-done.4), kind=kLoop, calls=%fused_computation.18 | loop fusion | flops 3744000 | bytes 1653760 | tf_op jit(solution)/shard_map/concatenate | solution.py:24
  23.6 0.0 copy-start.1
  23.6 0.2 slice_bitcast_fusion.11
  23.8 0.0 copy-start.2
  23.8 0.8 multiply_bitcast_fusion.8
  24.7 0.0 copy-done.1
  24.7 1.0 fusion.79
  25.7 0.2 fusion.40
  25.9 1.0 fusion.34
  26.9 0.5 fusion.15
  27.4 2.5 %fusion.7 = f32[4,8,4,2,4,128,1]{5,1,6,4,3,2,0:T(8,128)S(1)} fusion(s32[8,128]{1,0:T(8,128)S(1)} %multiply_add_fusion.5, s32[2,4,128]{2,1,0:T(4,128)S(1)} %add_add_fusion, f32[4,8,8,4,128]{4,1,0,3,2:T(8,128)S(1)} %fusion.15), kind=kOutput, calls=%fused_computation.6 | convolution fusion | flops 1611792384 | bytes 1056768 | tf_op jit(solution)/shard_map/dot_general | solution.py:108
  29.9 0.2 copy_add_fusion.1
  30.1 1.3 %collective-permute-start.6 = (f32[4,8,1,4,128]{4,3,2,1,0:T(4,128)S(1)}, f32[4,8,1,4,128]{4,3,2,1,0:T(4,128)S(1)}, u32[]{:S(2)}, u32[]{:S(2)}) collective-permute-start(f32[4,8,1,4,128]{4,3,2,1,0:T(4,128)S(1)} %get-tuple-element.29), channel_id=1, source_target_pairs={{8,0},{16,8},{24,16},{9,1},{17,9},{25,17},{10,2},{18,10},{26,18},{... | collective-permute-start | bytes 196616 | tf_op jit(solution)/shard_map/ppermute | solution.py:23
  31.4 5.4 %collective-permute-start.7 = (f32[4,8,1,4,128]{4,3,2,1,0:T(4,128)S(1)}, f32[4,8,1,4,128]{4,3,2,1,0:T(4,128)S(1)}, u32[]{:S(2)}, u32[]{:S(2)}) collective-permute-start(f32[4,8,1,4,128]{4,3,2,1,0:T(4,128)S(1)} %get-tuple-element.28), channel_id=1, source_target_pairs={{0,8},{8,16},{16,24},{1,9},{9,17},{17,25},{2,10},{10,18},{18,26},{... | collective-permute-start | bytes 196616 | tf_op jit(solution)/shard_map/ppermute | solution.py:22
  37.0 4.1 %collective-permute-start.5 = (f32[3,8,4,128]{3,2,1,0:T(4,128)S(1)}, f32[3,8,4,128]{3,2,1,0:T(4,128)S(1)}, u32[]{:S(2)}, u32[]{:S(2)}) collective-permute-start(f32[3,8,4,128]{3,2,1,0:T(4,128)S(1)} %slice_bitcast_fusion.13), channel_id=1, source_target_pairs={{0,1},{1,2},{2,3},{3,4},{4,5},{5,6},{6,7},{8,9},{9,10},{10,11},{11... | collective-permute-start | bytes 147464 | tf_op jit(solution)/shard_map/ppermute | solution.py:31
  41.1 0.8 select_maximum_fusion.2
  41.9 0.2 slice_bitcast_fusion.7
  42.1 0.8 multiply_bitcast_fusion.5
  42.9 1.0 fusion.64
  43.8 0.2 fusion.41
  44.1 1.0 fusion.37
  45.1 0.5 fusion.14
  45.6 2.5 %fusion.5 = f32[4,8,4,2,4,128,1]{5,1,6,4,3,2,0:T(8,128)S(1)} fusion(s32[8,128]{1,0:T(8,128)S(1)} %multiply_add_fusion.5, s32[2,4,128]{2,1,0:T(4,128)S(1)} %add_add_fusion, f32[4,8,8,4,128]{4,1,0,3,2:T(8,128)S(1)} %fusion.14), kind=kOutput, calls=%fused_computation.4 | convolution fusion | flops 1611792384 | bytes 1056768 | tf_op jit(solution)/shard_map/dot_general | solution.py:108
  48.1 0.2 copy_add_fusion
  48.3 0.0 copy-start
  48.4 4.5 %collective-permute-start.10 = (f32[4,8,1,4,128]{4,3,2,1,0:T(4,128)S(1)}, f32[4,8,1,4,128]{4,3,2,1,0:T(4,128)S(1)}, u32[]{:S(2)}, u32[]{:S(2)}) collective-permute-start(f32[4,8,1,4,128]{4,3,2,1,0:T(4,128)S(1)} %get-tuple-element.26), channel_id=1, source_target_pairs={{0,8},{8,16},{16,24},{1,9},{9,17},{17,25},{2,10},{10,18},{18,26},{... | collective-permute-start | bytes 196616 | tf_op jit(solution)/shard_map/ppermute | solution.py:22
  52.9 1.3 %collective-permute-start.9 = (f32[4,8,1,4,128]{4,3,2,1,0:T(4,128)S(1)}, f32[4,8,1,4,128]{4,3,2,1,0:T(4,128)S(1)}, u32[]{:S(2)}, u32[]{:S(2)}) collective-permute-start(f32[4,8,1,4,128]{4,3,2,1,0:T(4,128)S(1)} %get-tuple-element.27), channel_id=1, source_target_pairs={{8,0},{16,8},{24,16},{9,1},{17,9},{25,17},{10,2},{18,10},{26,18},{... | collective-permute-start | bytes 196616 | tf_op jit(solution)/shard_map/ppermute | solution.py:23
  54.2 2.4 %collective-permute-start.8 = (f32[3,8,4,128]{3,2,1,0:T(4,128)S(1)}, f32[3,8,4,128]{3,2,1,0:T(4,128)S(1)}, u32[]{:S(2)}, u32[]{:S(2)}) collective-permute-start(f32[3,8,4,128]{3,2,1,0:T(4,128)S(1)} %slice_bitcast_fusion.12), channel_id=1, source_target_pairs={{0,1},{1,2},{2,3},{3,4},{4,5},{5,6},{6,7},{8,9},{9,10},{10,11},{11... | collective-permute-start | bytes 147464 | tf_op jit(solution)/shard_map/ppermute | solution.py:31
  56.7 2.4 %collective-permute-done.9 = f32[4,8,1,4,128]{4,3,2,1,0:T(4,128)S(1)} collective-permute-done((f32[4,8,1,4,128]{4,3,2,1,0:T(4,128)S(1)}, f32[4,8,1,4,128]{4,3,2,1,0:T(4,128)S(1)}, u32[]{:S(2)}, u32[]{:S(2)}) %collective-permute-start.9) | collective-permute-done | bytes 65568 | tf_op jit(solution)/shard_map/ppermute | solution.py:23
  59.1 0.8 select_maximum_fusion
  59.9 0.2 slice_bitcast_fusion.3
  60.0 0.8 multiply_bitcast_fusion.2
  60.9 1.0 fusion.49
  61.9 0.2 maximum_subtract_fusion.2
  62.1 5.8 %copy.46 = f32[4,8,8,4,128]{1,0,4,3,2:T(4,128)} copy(f32[4,8,8,4,128]{4,3,2,1,0:T(4,128)S(1)} %maximum_subtract_fusion.2) | data formatting | bytes 1048576 | tf_op jit(solution)/shard_map/sub | solution.py:133
  67.9 11.4 %reshape.264 = f32[8,1,16384]{2,1,0:T(1,128)S(1)} reshape(f32[4096,4,8]{2,1,0:T(4,128)} %bitcast.157) | data formatting | bytes 1048576
  79.3 20.4 %all_to_all.18 = f32[8,1,16384]{2,1,0:T(1,128)S(1)} all-to-all(f32[8,1,16384]{2,1,0:T(1,128)S(1)} %reshape.264), channel_id=1, replica_groups=mesh['space'=4,'tm'=8] {'tm'}, dimensions={0} | all-to-all | bytes 1048576 | tf_op jit(solution)/shard_map/all_to_all | solution.py:140
  99.7 0.5 broadcast.416
  100.2 1.9 %reduce.4 = f32[8,16384]{1,0:T(8,128)S(1)} reduce(f32[8,1,16384]{2,1,0:T(1,128)S(1)} %all_to_all.18, f32[]{:T(128)} %broadcast.416), dimensions={1}, to_apply=%all_to_all.13.reduce_sub_computation | reduce | bytes 1048580 | tf_op jit(solution)/shard_map/all_to_all | solution.py:140
  102.1 13.1 %reshape.265 = f32[4096,4,8]{2,1,0:T(4,128)} reshape(f32[8,16384]{1,0:T(8,128)S(1)} %reduce.4) | data formatting | bytes 1048576
  115.2 6.6 %copy.47 = f32[4,8,8,512]{3,2,1,0:T(8,128)S(1)} copy(f32[4,8,8,512]{2,0,3,1:T(4,128)} %bitcast.158) | data formatting | bytes 1048576 | tf_op jit(solution)/shard_map/all_to_all | solution.py:140
  121.9 0.1 slice.562
  122.0 0.1 slice.564
  122.2 0.1 multiply_add_fusion
  122.7 0.6 multiply_add_fusion.4
  (40 shorter events, 0.6 us)
Async XLA Ops:
  1.5 20.3 %collective-permute-start.2 = (f32[4,8,1,4,128]{4,3,2,1,0:T(4,128)S(1)}, f32[4,8,1,4,128]{4,3,2,1,0:T(4,128)S(1)}, u32[]{:S(2)}, u32[]{:S(2)}) collective-permute-start(f32[4,8,1,4,128]{4,3,2,1,0:T(4,128)S(1)} %get-tuple-element.31), channel_id=1, source_target_pairs={{8,0},{16,8},{24,16},{9,1},{17,9},{25,17},{10,2},{18,10},{26,18},{... | collective-permute-start | bytes 196616 | tf_op jit(solution)/shard_map/ppermute | solution.py:23
  2.8 19.0 %collective-permute-start.4 = (f32[4,8,1,4,128]{4,3,2,1,0:T(4,128)S(1)}, f32[4,8,1,4,128]{4,3,2,1,0:T(4,128)S(1)}, u32[]{:S(2)}, u32[]{:S(2)}) collective-permute-start(f32[4,8,1,4,128]{4,3,2,1,0:T(4,128)S(1)} %get-tuple-element.30), channel_id=1, source_target_pairs={{0,8},{8,16},{16,24},{1,9},{9,17},{17,25},{2,10},{10,18},{18,26},{... | collective-permute-start | bytes 196616 | tf_op jit(solution)/shard_map/ppermute | solution.py:22
  9.8 11.7 %collective-permute-start.1 = (f32[1,4,128]{2,0,1:T(1,128)S(1)}, f32[1,4,128]{2,0,1:T(1,128)S(1)}, u32[]{:S(2)}, u32[]{:S(2)}) collective-permute-start(f32[1,4,128]{2,0,1:T(1,128)S(1)} %get-tuple-element.39), channel_id=1, source_target_pairs={{8,0},{16,8},{24,16},{9,1},{17,9},{25,17},{10,2},{18,10},{26,18},{... | collective-permute-start | bytes 6152 | tf_op jit(solution)/shard_map/ppermute | solution.py:23
  11.1 10.4 %collective-permute-start.3 = (f32[1,4,128]{2,0,1:T(1,128)S(1)}, f32[1,4,128]{2,0,1:T(1,128)S(1)}, u32[]{:S(2)}, u32[]{:S(2)}) collective-permute-start(f32[1,4,128]{2,0,1:T(1,128)S(1)} %get-tuple-element.38), channel_id=1, source_target_pairs={{0,8},{8,16},{16,24},{1,9},{9,17},{17,25},{2,10},{10,18},{18,26},{... | collective-permute-start | bytes 6152 | tf_op jit(solution)/shard_map/ppermute | solution.py:22
  17.3 7.3 %collective-permute-start = (f32[3,8,4,128]{3,2,1,0:T(4,128)S(1)}, f32[3,8,4,128]{3,2,1,0:T(4,128)S(1)}, u32[]{:S(2)}, u32[]{:S(2)}) collective-permute-start(f32[3,8,4,128]{3,2,1,0:T(4,128)S(1)} %slice_bitcast_fusion.14), channel_id=1, source_target_pairs={{0,1},{1,2},{2,3},{3,4},{4,5},{5,6},{6,7},{8,9},{9,10},{10,11},{11... | collective-permute-start | bytes 147464 | tf_op jit(solution)/shard_map/ppermute | solution.py:31
  23.6 1.0 copy-start.1
  23.8 1.8 %copy-start.2 = (f32[4,8,8,4,128]{4,3,2,1,0:T(4,128)S(1)}, f32[4,8,8,4,128]{4,3,2,1,0:T(4,128)}, u32[]{:S(2)}) copy-start(f32[4,8,8,4,128]{4,3,2,1,0:T(4,128)} %param.7) | copy-start | bytes 1572868
  30.1 10.9 %collective-permute-start.6 = (f32[4,8,1,4,128]{4,3,2,1,0:T(4,128)S(1)}, f32[4,8,1,4,128]{4,3,2,1,0:T(4,128)S(1)}, u32[]{:S(2)}, u32[]{:S(2)}) collective-permute-start(f32[4,8,1,4,128]{4,3,2,1,0:T(4,128)S(1)} %get-tuple-element.29), channel_id=1, source_target_pairs={{8,0},{16,8},{24,16},{9,1},{17,9},{25,17},{10,2},{18,10},{26,18},{... | collective-permute-start | bytes 196616 | tf_op jit(solution)/shard_map/ppermute | solution.py:23
  31.4 9.6 %collective-permute-start.7 = (f32[4,8,1,4,128]{4,3,2,1,0:T(4,128)S(1)}, f32[4,8,1,4,128]{4,3,2,1,0:T(4,128)S(1)}, u32[]{:S(2)}, u32[]{:S(2)}) collective-permute-start(f32[4,8,1,4,128]{4,3,2,1,0:T(4,128)S(1)} %get-tuple-element.28), channel_id=1, source_target_pairs={{0,8},{8,16},{16,24},{1,9},{9,17},{17,25},{2,10},{10,18},{18,26},{... | collective-permute-start | bytes 196616 | tf_op jit(solution)/shard_map/ppermute | solution.py:22
  37.0 5.9 %collective-permute-start.5 = (f32[3,8,4,128]{3,2,1,0:T(4,128)S(1)}, f32[3,8,4,128]{3,2,1,0:T(4,128)S(1)}, u32[]{:S(2)}, u32[]{:S(2)}) collective-permute-start(f32[3,8,4,128]{3,2,1,0:T(4,128)S(1)} %slice_bitcast_fusion.13), channel_id=1, source_target_pairs={{0,1},{1,2},{2,3},{3,4},{4,5},{5,6},{6,7},{8,9},{9,10},{10,11},{11... | collective-permute-start | bytes 147464 | tf_op jit(solution)/shard_map/ppermute | solution.py:31
  48.3 12.6 %copy-start = (f32[4,8,8,4,128]{4,3,2,1,0:T(4,128)}, f32[4,8,8,4,128]{4,3,2,1,0:T(4,128)S(1)}, u32[]{:S(2)}) copy-start(f32[4,8,8,4,128]{4,3,2,1,0:T(4,128)S(1)} %copy_add_fusion) | copy-start | bytes 1572868
  48.4 8.3 %collective-permute-start.10 = (f32[4,8,1,4,128]{4,3,2,1,0:T(4,128)S(1)}, f32[4,8,1,4,128]{4,3,2,1,0:T(4,128)S(1)}, u32[]{:S(2)}, u32[]{:S(2)}) collective-permute-start(f32[4,8,1,4,128]{4,3,2,1,0:T(4,128)S(1)} %get-tuple-element.26), channel_id=1, source_target_pairs={{0,8},{8,16},{16,24},{1,9},{9,17},{17,25},{2,10},{10,18},{18,26},{... | collective-permute-start | bytes 196616 | tf_op jit(solution)/shard_map/ppermute | solution.py:22
  52.9 6.2 %collective-permute-start.9 = (f32[4,8,1,4,128]{4,3,2,1,0:T(4,128)S(1)}, f32[4,8,1,4,128]{4,3,2,1,0:T(4,128)S(1)}, u32[]{:S(2)}, u32[]{:S(2)}) collective-permute-start(f32[4,8,1,4,128]{4,3,2,1,0:T(4,128)S(1)} %get-tuple-element.27), channel_id=1, source_target_pairs={{8,0},{16,8},{24,16},{9,1},{17,9},{25,17},{10,2},{18,10},{26,18},{... | collective-permute-start | bytes 196616 | tf_op jit(solution)/shard_map/ppermute | solution.py:23
  54.2 6.6 %collective-permute-start.8 = (f32[3,8,4,128]{3,2,1,0:T(4,128)S(1)}, f32[3,8,4,128]{3,2,1,0:T(4,128)S(1)}, u32[]{:S(2)}, u32[]{:S(2)}) collective-permute-start(f32[3,8,4,128]{3,2,1,0:T(4,128)S(1)} %slice_bitcast_fusion.12), channel_id=1, source_target_pairs={{0,1},{1,2},{2,3},{3,4},{4,5},{5,6},{6,7},{8,9},{9,10},{10,11},{11... | collective-permute-start | bytes 147464 | tf_op jit(solution)/shard_map/ppermute | solution.py:31
where the time goes:
time: 124 us; the launch traced here: 123 us
  local copies, waits for them, and re-layouts  43.8 us (35%)
  starting transfers between devices  33.9 us (27%)
  blocking collectives  20.4 us (16%)
  other arithmetic  13.5 us (11%)
  matrix products  8.04 us (6%)
  waiting for transfers between devices  2.43 us (2%)
  between operations  1.27 us (1%)
    unnamed x9, local copies, waits for them, and re-layouts  25.3 us
    ppermute x4, starting transfers between devices, extended_2(): before = lax.ppermute(last, axis, up)  20.9 us
    all_to_all x1, blocking collectives, per_device(): lax.all_to_all(flattened, 'tm', split_axis=2, concat_axis=1, tiled=True)  20.4 us
    ppermute x3, starting transfers between devices, passed_along(): return lax.ppermute(shard, axis, pairs)  7.82 us
    all_to_all x2, local copies, waits for them, and re-layouts, per_device(): lax.all_to_all(flattened, 'tm', split_axis=2, concat_axis=1, tiled=True)  7.16 us
    sub x1, local copies, waits for them, and re-layouts, residual_of(): return forcing - operate(padded, earlier, visc_pad)  5.83 us
    ppermute x4, starting transfers between devices, extended_2(): after = lax.ppermute(leading, axis, down)  5.17 us
    dot_general x2, matrix products, vanka_patches(): lax.dot_general(scaled, back_table, (((1, 5), (3, 4)), ((), ())), precisi...  5.04 us
  transfers between devices with their start and end apart: 11, of which 1 were waited for; matrix products, arithmetic and copies ran while one was open for 9% of the time, Pallas kernels for 0%

commit v1 on v0

v1 whole, which is shorter than its diff:
```python
import functools

import jax
import jax.numpy as jnp
from jax import lax
from jax.experimental import pallas as pl
from jax.experimental.pallas import tpu as pltpu
from jax.sharding import PartitionSpec as P

SWEEPS = 2
LEVELS = 5
FACTOR = 2**LEVELS

damping = 0.8
stabilize = 0.1

F32 = jnp.float32
BF16 = jnp.bfloat16

TILE = 8
PLANE = 4


def hat(step, k):
    far = step - FACTOR * k
    far = jnp.where(far < 0, -far, far)
    return jnp.where(far < FACTOR, FACTOR - far, 0).astype(F32) * (1.0 / FACTOR**2)


def lane_ids(shape):
    return lax.broadcasted_iota(jnp.int32, shape, 1)


def row_ids(shape):
    return lax.broadcasted_iota(jnp.int32, shape, 0)


def rolled(tile, by):
    return pltpu.roll(tile, by % tile.shape[1], 1)


def edge_masks():
    shape = (TILE, 128)
    row = row_ids(shape) % PLANE
    lane = lane_ids(shape)
    one = lambda keep: jnp.where(keep, 1.0, 0.0).astype(F32)
    return one(row < PLANE - 1), one(row > 0), one(lane < 127), one(lane > 0)


def coefficients(visc_pad, base, masks):
    v = visc_pad[base : base + 8]
    around = (
        visc_pad[base + 4 : base + 12],
        visc_pad[base - 4 : base + 4],
        masks[0] * visc_pad[base + 1 : base + 9],
        masks[1] * visc_pad[base - 1 : base + 7],
        masks[2] * rolled(v, -1),
        masks[3] * rolled(v, 1),
    )
    kappas = [0.5 * (v + other) for other in around]
    diagonal = sum(kappas[1:], kappas[0])
    kept = kappas[:2] + [mask * kappa for mask, kappa in zip(masks, kappas[2:])]
    return diagonal, kept


def neighbours(at, base, masks=None):
    centre = at(base)
    y_up, y_down = at(base + 1), at(base - 1)
    z_up, z_down = rolled(centre, -1), rolled(centre, 1)
    if masks is not None:
        y_up, y_down, z_up, z_down = (
            masks[0] * y_up,
            masks[1] * y_down,
            masks[2] * z_up,
            masks[3] * z_down,
        )
    return centre, (at(base + 4), at(base - 4), y_up, y_down, z_up, z_down)


def space_operator(ats, base, coefs, masks):
    diagonal, kappas = coefs
    pressure, beside = neighbours(ats[3], base, masks)
    total = sum(beside[1:], beside[0])
    out = []
    divergence = None
    for c in range(3):
        centre, near = neighbours(ats[c], base)
        spread = sum((k * f for k, f in zip(kappas[1:], near[1:])), kappas[0] * near[0])
        slope = 0.5 * (beside[2 * c] - beside[2 * c + 1])
        out.append(diagonal * centre - spread + slope)
        up, down = near[2 * c], near[2 * c + 1]
        if c > 0:
            up, down = masks[2 * c - 2] * up, masks[2 * c - 1] * down
        part = up - down
        divergence = part if divergence is None else divergence + part
    out.append(stabilize * (6.0 * pressure - total) - 0.5 * divergence)
    return out


def residual(ats, before, forcing, base, coefs, masks):
    applied = space_operator(ats, base, coefs, masks)
    out = []
    for c in range(3):
        out.append(forcing[c] - (ats[c](base) - before[c]) - applied[c])
    out.append(forcing[3] - applied[3])
    return out


def kind_masks(kind_tile, kinds):
    out = []
    for k in range(kinds):
        mask = jnp.where(kind_tile == float(k), 1.0, 0.0).astype(F32)
        out.append(jnp.concatenate([mask] * 8, axis=0).astype(BF16))
    return out


def put_operand(x_ref, at, tiles, masks):
    same = jnp.concatenate(tiles, axis=0)
    even = lane_ids(same.shape) % 2 == 0
    other = jnp.where(even, rolled(same, -1), rolled(same, 1))
    both = jnp.concatenate([same, other], axis=0).astype(BF16)
    for k, mask in enumerate(masks):
        x_ref[64 * k : 64 * k + 64, 128 * at : 128 * at + 128] = both * mask


def patch_product(w_ref, x_ref, count):
    return jnp.dot(w_ref[...], x_ref[:, : 128 * count], preferred_element_type=F32)


def taken(product, at):
    first = product[:32, 128 * at : 128 * at + 128]
    second = product[32:, 128 * at : 128 * at + 128]
    chosen = jnp.where(lane_ids(first.shape) % 2 == 0, first, second)
    return [damping * chosen[8 * c : 8 * c + 8] for c in range(4)]


def side_slots():
    odd = lax.axis_index("space") % 2
    return odd ^ 1, odd


def tiles_at(ref, n):
    return [lambda row, c=c: ref[c, n, row : row + 8] for c in range(4)]


def tables_kernel(table_ref, class_ref, bank_ref, kind_ref, visc_ref, kinds_ref, w_ref, rows_ref):
    planes = class_ref.shape[0]
    for x in range(planes):
        classes = class_ref[x]
        found = jnp.zeros(classes.shape, F32)
        for k in range(table_ref.shape[0]):
            found = jnp.where(classes == k, table_ref[k], found)
        visc_ref[PLANE * x : PLANE * x + PLANE] = found

    groups = kind_ref.shape[0]
    for g in range(groups):
        rows_ref[2 * g : 2 * g + 2] = kind_ref[g].astype(F32)
    rows = PLANE * planes
    shape = (rows, 2 * groups)
    r = row_ids(shape)
    spread_rows = jnp.where(lane_ids(shape) == r // 8 * 2 + r % 4 // 2, 1.0, 0.0).astype(BF16)
    shape = (64, 128)
    spread_lanes = jnp.where(row_ids(shape) == lane_ids(shape) // 2, 1.0, 0.0).astype(BF16)
    wide = jnp.dot(rows_ref[...].astype(BF16), spread_lanes, preferred_element_type=F32)
    kinds_ref[...] = jnp.dot(spread_rows, wide.astype(BF16), preferred_element_type=F32)

    shape = (32, 64)
    same_y = row_ids(shape) // 2 % 2 == lane_ids(shape) // 2 % 2
    for p in range(2):
        shape = (32, 32)
        r = row_ids(shape)
        left = jnp.where(lane_ids(shape) == r // 4 * 4 + r % 2 * 2 + p, 1.0, 0.0).astype(BF16)
        shape = (32, 64)
        q = lane_ids(shape)
        side = (p + q // 32) % 2
        at = q % 32
        right = jnp.where(row_ids(shape) == at // 4 * 4 + at % 2 * 2 + side, 1.0, 0.0).astype(BF16)
        for k in range(bank_ref.shape[0]):
            half = jnp.dot(bank_ref[k], right, preferred_element_type=F32).astype(BF16)
            full = jnp.dot(left, half, preferred_element_type=F32)
            w_ref[32 * p : 32 * p + 32, 64 * k : 64 * k + 64] = jnp.where(same_y, full, 0.0).astype(BF16)


def tail_kernel(guess_ref, forcing_ref, out_ref):
    out_ref[:, 0] = guess_ref[:, 1]
    out_ref[0:3, 1] = forcing_ref[0:3, 0] + guess_ref[0:3, 0]
    out_ref[3, 1] = forcing_ref[3, 0]


def first_message_kernel(low_ref, high_ref, t_low_ref, t_high_ref, visc_ref, kinds_ref, a_ref, b_ref):
    steps = low_ref.shape[1]
    rows = visc_ref.shape[0]
    left, _ = side_slots()

    def fill(to_left, to_right):
        for ref, edge, t_edge, first, row in (
            (to_left, low_ref, t_low_ref, 0, 0),
            (to_right, high_ref, t_high_ref, 4, rows - 4),
        ):
            for c in range(4):
                at = c * (steps + 1) * 4
                ref[at : at + 4] = t_edge[c, 0, first : first + 4]
                for n in range(steps):
                    ref[at + 4 + 4 * n : at + 8 + 4 * n] = edge[c, n, first : first + 4]
            at = 16 * (steps + 1)
            ref[at : at + 4] = visc_ref[row : row + 4]
            ref[at + 4 : at + 8] = kinds_ref[row : row + 4]

    @pl.when(left == 0)
    def _():
        fill(a_ref, b_ref)

    @pl.when(left == 1)
    def _():
        fill(b_ref, a_ref)


def first_sweep(g, offset, ats, guess, guess_ref, forcing_ref, t_ref, coefs, masks, kinds_ref, w_ref, x_ref, put):
    steps = forcing_ref.shape[1]
    base = offset + TILE * g
    own = slice(TILE * g, TILE * g + TILE)
    chosen = kind_masks(kinds_ref[own], w_ref.shape[1] // 64)
    for n in range(-1, steps):
        if n < 0:
            applied = space_operator(ats(n), base, coefs, masks)
            tiles = [t_ref[c, 1, own] - (t_ref[c, 0, own] if c < 3 else 0.0) - applied[c] for c in range(4)]
        else:
            force = [forcing_ref[c, n, own] for c in range(4)]
            before = [t_ref[c, 0, own] if n == 0 else guess_ref[c, n - 1, own] for c in range(3)]
            tiles = residual(ats(n), before, force, base, coefs, masks)
        put_operand(x_ref, n + 1, tiles, chosen)
    product = patch_product(w_ref, x_ref, steps + 1)
    for n in range(-1, steps):
        change = taken(product, n + 1)
        put(n, own, [guess(c, n, own) + change[c] for c in range(4)])


def first_inner_kernel(guess_ref, forcing_ref, t_ref, visc_ref, kinds_ref, w_ref, inner_ref, x_ref):
    rows = guess_ref.shape[2]
    masks = edge_masks()

    def ats(n):
        return tiles_at(t_ref, 0) if n < 0 else tiles_at(guess_ref, n)

    def guess(c, n, own):
        return t_ref[c, 0, own] if n < 0 else guess_ref[c, n, own]

    def put(n, own, values):
        for c in range(4):
            inner_ref[c, n + 1, own.start - TILE : own.stop - TILE] = values[c]

    for g in range(1, rows // TILE - 1):
        coefs = coefficients(visc_ref, TILE * g, masks)
        first_sweep(
            g, 0, ats, guess, guess_ref, forcing_ref, t_ref, coefs, masks, kinds_ref, w_ref, x_ref, put
        )


def by_side(which, work):
    left, _ = side_slots()

    @pl.when(left == which)
    def _():
        work(0)

    @pl.when(left != which)
    def _():
        work(1)


def local_rows(side, rows):
    if side == 0:
        return slice(8, 20), slice(0, 12)
    return slice(4, 16), slice(rows - 12, rows)


def first_side_kernel(
    guess_ref,
    forcing_ref,
    t_ref,
    inner_ref,
    in_ref,
    visc_ref,
    kinds_ref,
    w_ref,
    *refs,
    which,
    coarse,
):
    if which:
        straight_ref, it_ref, out_ref, visc_loc, passed_ref, u_ref, v_ref, x_ref = refs
        passed_ref[...] = straight_ref[...]
    else:
        it_ref, out_ref, visc_loc, u_ref, v_ref, x_ref = refs
    steps, rows = guess_ref.shape[1], guess_ref.shape[2]
    start = lax.axis_index("tm") * steps
    masks = edge_masks()
    weights = [[hat(start + n, k) for n in range(steps)] for k in range(coarse)]
    count = 16 * steps

    def work(side):
        g = 0 if side == 0 else rows // TILE - 1
        own = slice(TILE * g, TILE * g + TILE)
        there, here = local_rows(side, rows)
        halo = slice(4, 8) if side == 0 else slice(16, 20)
        u_ref[:, 0, there] = t_ref[:, 0, here]
        u_ref[:, 1 : 1 + steps, there] = guess_ref[:, :, here]
        for c in range(4):
            for n in range(steps + 1):
                at = (c * (steps + 1) + n) * 4
                u_ref[c, n, halo] = in_ref[at : at + 4]
        at = 16 * (steps + 1)
        visc_loc[there] = visc_ref[here]
        visc_loc[halo] = in_ref[at : at + 4]
        coefs = coefficients(visc_loc, 8, masks)

        def ats(n):
            return tiles_at(u_ref, n + 1)

        def guess(c, n, own):
            return u_ref[c, n + 1, 8:16]

        def put(n, own, values):
            for c in range(4):
                it_ref[c, n + 1] = values[c]

        first_sweep(
            g, 8 - TILE * g, ats, guess, guess_ref, forcing_ref, t_ref, coefs, masks, kinds_ref, w_ref, x_ref, put
        )

        v_ref[:, :, halo] = jnp.zeros((4, steps, 4, 128), F32)
        v_ref[:, :, 8:16] = it_ref[:, 1:]
        if side == 0:
            v_ref[:, :, 16:20] = inner_ref[:, 1:, 0:4]
        else:
            v_ref[:, :, 4:8] = inner_ref[:, 1:, rows - 2 * TILE - 4 : rows - 2 * TILE]
        edge, inner = (0, 4) if side == 0 else (4, 0)
        sums = [[None] * coarse for _ in range(4)]
        for n in range(steps):
            force = [forcing_ref[c, n, own] for c in range(4)]
            before = [it_ref[c, n] for c in range(3)]
            tiles = residual(tiles_at(v_ref, n), before, force, 8, coefs, masks)
            for c in range(4):
                at = (c * steps + n) * 4
                out_ref[at : at + 4] = v_ref[c, n, 8 + edge : 12 + edge]
                out_ref[count + at : count + at + 4] = tiles[c][edge : edge + 4]
                rounded = tiles[c].astype(BF16).astype(F32)
                for k in range(coarse):
                    part = weights[k][n] * rounded
                    sums[c][k] = part if n == 0 else sums[c][k] + part
        for c in range(4):
            for k in range(coarse):
                at = 2 * count + (c * coarse + k) * 4
                out_ref[at : at + 4] = sums[c][k][inner : inner + 4]

    by_side(which, work)


class Restriction:
    def __init__(self, weights, forcing_ref, smooth_ref, shift):
        self.weights, self.forcing_ref, self.smooth_ref, self.shift = weights, forcing_ref, smooth_ref, shift
        self.held = [[None] * len(weights) for _ in range(4)]
        self.rest = [[None] * len(weights) for _ in range(4)]

    def put(self, n, own, values):
        for c in range(4):
            self.smooth_ref[c, n, own.start + self.shift : own.stop + self.shift] = values[c]
            force = self.forcing_ref[c, n, own]
            for k, weight in enumerate(self.weights):
                one, two = weight[n] * values[c], weight[n] * force
                if c < 3:
                    two = two - (weight[n] - weight[n + 1]) * values[c]
                self.held[c][k] = one if n == 0 else self.held[c][k] + one
                self.rest[c][k] = two if n == 0 else self.rest[c][k] + two


def block_weights(steps, coarse):
    start = lax.axis_index("tm") * steps
    return [[hat(start + n, k) for n in range(steps + 1)] for k in range(coarse)]


def second_sweep(g, offset, u_ref, shift, it_ref, it_own, forcing_ref, coefs, masks, kinds_ref, w_ref, x_ref, put):
    steps = forcing_ref.shape[1]
    base = offset + TILE * g
    own = slice(TILE * g, TILE * g + TILE)
    chosen = kind_masks(kinds_ref[own], w_ref.shape[1] // 64)
    for n in range(steps):
        force = [forcing_ref[c, n, own] for c in range(4)]
        before = [it_ref[c, n, it_own] for c in range(3)]
        put_operand(x_ref, n, residual(tiles_at(u_ref, n + shift), before, force, base, coefs, masks), chosen)
    product = patch_product(w_ref, x_ref, steps)
    for n in range(steps):
        change = taken(product, n)
        put(n, own, [it_ref[c, n + 1, it_own] + change[c] for c in range(4)])


def second_inner_kernel(
    a_ref, b_ref, inner_ref, forcing_ref, visc_ref, kinds_ref, w_ref, smooth_ref, sums_ref, it_ref, x_ref
):
    steps, rows = forcing_ref.shape[1], forcing_ref.shape[2]
    coarse = sums_ref.shape[3]
    masks = edge_masks()
    weights = block_weights(steps, coarse)
    it_ref[:, :, TILE : rows - TILE] = inner_ref[...]

    def work(side):
        low, high = (a_ref, b_ref) if side == 0 else (b_ref, a_ref)
        it_ref[:, :, 0:TILE] = low[...]
        it_ref[:, :, rows - TILE : rows] = high[...]

    by_side(0, work)
    for g in range(1, rows // TILE - 1):
        sums = Restriction(weights, forcing_ref, smooth_ref, -TILE)
        coefs = coefficients(visc_ref, TILE * g, masks)
        own = slice(TILE * g, TILE * g + TILE)
        second_sweep(
            g, 0, it_ref, 1, it_ref, own, forcing_ref, coefs, masks, kinds_ref, w_ref, x_ref, sums.put
        )
        for c in range(4):
            for k in range(coarse):
                sums_ref[g - 1, 0, c, k] = sums.held[c][k]
                sums_ref[g - 1, 1, c, k] = sums.rest[c][k]


def second_side_kernel(
    it_ref,
    inner_ref,
    forcing_ref,
    first_ref,
    in_ref,
    visc_loc,
    kinds_ref,
    w_ref,
    after_ref,
    smooth_ref,
    sums_ref,
    halo_ref,
    v_ref,
    x_ref,
    *,
    which,
):
    steps, rows = forcing_ref.shape[1], forcing_ref.shape[2]
    coarse = sums_ref.shape[2]
    kinds = w_ref.shape[1] // 64
    space = lax.axis_index("space")
    count = 16 * steps
    static = 16 * (steps + 1)
    masks = edge_masks()
    weights = block_weights(steps, coarse)

    def work(side):
        g = 0 if side == 0 else rows // TILE - 1
        if side == 0:
            inside, outer, edge, sign = 8, 4, 4, 1.0
            exists = space > 0
            v_ref[:, :, 16:20] = inner_ref[:, 1:, 0:4]
        else:
            inside, outer, edge, sign = 12, 16, 0, -1.0
            exists = space < lax.axis_size("space") - 1
            v_ref[:, :, 4:8] = inner_ref[:, 1:, rows - 2 * TILE - 4 : rows - 2 * TILE]
        v_ref[:, :, 8:16] = it_ref[:, 1:]
        for c in range(4):
            for n in range(steps):
                at = (c * steps + n) * 4
                v_ref[c, n, outer : outer + 4] = in_ref[at : at + 4]

        kappa = 0.5 * (visc_loc[inside : inside + 4] + visc_loc[outer : outer + 4])
        sums = [[None] * coarse for _ in range(4)]
        plain = [[None] * coarse for _ in range(4)]
        for n in range(steps):
            mine = [v_ref[c, n, inside : inside + 4] for c in range(4)]
            add = [kappa * mine[c] for c in range(3)]
            add[0] = add[0] - (0.5 * sign) * mine[3]
            add.append(stabilize * mine[3] + (0.5 * sign) * mine[0])
            for c in range(4):
                at = count + (c * steps + n) * 4
                rounded = (in_ref[at : at + 4] + add[c]).astype(BF16).astype(F32)
                value = v_ref[c, n, outer : outer + 4]
                for k in range(coarse):
                    one, two = weights[k][n] * rounded, weights[k][n] * value
                    sums[c][k] = one if n == 0 else sums[c][k] + one
                    plain[c][k] = two if n == 0 else plain[c][k] + two
        beside = first_ref[static + 4 : static + 8]
        chosen = kind_masks(jnp.concatenate([beside] * 2, axis=0), kinds)
        for k in range(coarse):
            tiles = []
            for c in range(4):
                at = 2 * count + (c * coarse + k) * 4
                far = in_ref[at : at + 4]
                pair = [far, sums[c][k]] if side == 0 else [sums[c][k], far]
                tiles.append(jnp.concatenate(pair, axis=0))
            high = [tile.astype(BF16).astype(F32) for tile in tiles]
            put_operand(x_ref, 2 * k, high, chosen)
            put_operand(x_ref, 2 * k + 1, [t - h for t, h in zip(tiles, high)], chosen)
        product = patch_product(w_ref, x_ref, 2 * coarse)
        exists = jnp.where(exists, 1.0, 0.0).astype(F32)
        for k in range(coarse):
            one, two = taken(product, 2 * k), taken(product, 2 * k + 1)
            for c in range(4):
                change = (one[c] + two[c])[edge : edge + 4]
                halo_ref[c, k] = exists * (plain[c][k] + change)

        totals = Restriction(weights, forcing_ref, smooth_ref, -TILE * g)
        coefs = coefficients(visc_loc, 8, masks)
        second_sweep(
            g, 8 - TILE * g, v_ref, 0, it_ref, slice(0, 8), forcing_ref, coefs, masks, kinds_ref, w_ref, x_ref, totals.put
        )
        for c in range(4):
            for k in range(coarse):
                sums_ref[0, c, k] = totals.held[c][k]
                sums_ref[1, c, k] = totals.rest[c][k]

    by_side(which, work)


def parts_kernel(
    a_sums_ref,
    b_sums_ref,
    a_halo_ref,
    b_halo_ref,
    a_visc_ref,
    b_visc_ref,
    inner_sums_ref,
    visc_ref,
    keep_ref,
    give_ref,
    s_ref,
    rest_ref,
    visc_pad,
    part_ref,
):
    size_t, _, coarse, share, _ = part_ref.shape
    rows = visc_ref.shape[0]
    groups = rows // TILE
    end = 8 + rows
    visc_pad[8:end] = visc_ref[...]
    s_ref[:, :, 16 : end - 8] = jnp.concatenate([inner_sums_ref[g, 0] for g in range(groups - 2)], axis=2)
    rest_ref[:, :, 8 : rows - 8] = jnp.concatenate([inner_sums_ref[g, 1] for g in range(groups - 2)], axis=2)

    def work(side):
        a = (a_sums_ref, a_halo_ref, a_visc_ref)
        b = (b_sums_ref, b_halo_ref, b_visc_ref)
        low, high = (a, b) if side == 0 else (b, a)
        s_ref[:, :, 8:16] = low[0][0]
        s_ref[:, :, end - 8 : end] = high[0][0]
        rest_ref[:, :, 0:8] = low[0][1]
        rest_ref[:, :, rows - 8 : rows] = high[0][1]
        s_ref[:, :, 4:8] = low[1][...]
        s_ref[:, :, end : end + 4] = high[1][...]
        visc_pad[4:8] = low[2][4:8]
        visc_pad[end : end + 4] = high[2][16:20]

    by_side(0, work)
    masks = edge_masks()
    for g in range(groups):
        base = 8 + TILE * g
        coefs = coefficients(visc_pad, base, masks)
        for k in range(coarse):
            applied = space_operator(tiles_at(s_ref, k), base, coefs, masks)
            for c in range(4):
                value = rest_ref[c, k, TILE * g : TILE * g + TILE] - applied[c]
                for row in range(0, TILE, share):
                    part_ref[(TILE * g + row) // share, c, k] = value[row : row + share]
    core = lax.axis_index("tm") % 2
    for i in range(size_t // 2):
        keep_ref[i] = part_ref[2 * i + core]
        give_ref[i] = part_ref[2 * i + (1 - core)]


def join_kernel(a_ref, b_ref, inner_ref, smooth_ref):
    rows = smooth_ref.shape[2]
    smooth_ref[:, :, TILE : rows - TILE] = inner_ref[...]

    def work(side):
        low, high = (a_ref, b_ref) if side == 0 else (b_ref, a_ref)
        smooth_ref[:, :, 0:TILE] = low[...]
        smooth_ref[:, :, rows - TILE : rows] = high[...]

    by_side(0, work)


def pair_kernel(keep_ref, given_ref, *refs, order):
    out_refs, sum_ref = refs[:-1], refs[-1]
    chip = lax.axis_index("tm") // 2
    sum_ref[...] = keep_ref[...] + given_ref[...]
    for d, ref in zip(order, out_refs):
        ref[...] = sum_ref[chip ^ d]


def total_kernel(*refs):
    out_ref = refs[-1]
    total = refs[0][...]
    for ref in refs[1:-1]:
        total = total + ref[...]
    for row in range(total.shape[2]):
        out_ref[:, :, 128 * row : 128 * row + 128] = total[:, :, row]


def whole_spec():
    return pl.BlockSpec(memory_space=pltpu.VMEM)


def call(kernel, outs, ins, scratch=(), specs=None, flops=10**6, limit=24, **options):
    size = sum(a.size * a.dtype.itemsize for a in ins)
    size += sum(o.size * o.dtype.itemsize for o in outs)
    return pl.pallas_call(
        kernel,
        out_shape=outs,
        in_specs=specs or [whole_spec()] * len(ins),
        out_specs=[whole_spec()] * len(outs),
        scratch_shapes=list(scratch),
        compiler_params=pltpu.CompilerParams(vmem_limit_bytes=int(limit * 2**20)),
        cost_estimate=pl.CostEstimate(flops=flops, bytes_accessed=size, transcendentals=0),
        **options,
    )(*ins)


def swapped(messages):
    size = lax.axis_size("space")
    out = []
    for number, message in enumerate(messages):
        pairs = [(i, i + 1) for i in range(number, size - 1, 2)]
        out.append(lax.ppermute(message, "space", pairs + [(j, i) for i, j in pairs]))
    return out


def shape_of(*dims, kind=F32):
    return jax.ShapeDtypeStruct(dims, kind)


def per_device(initial_guess, forcing, visc_table, visc_class, inverse_bank, patch_kind):
    comps, steps, planes, ny, nz = initial_guess.shape
    rows = planes * ny
    guess = initial_guess.reshape(comps, steps, rows, nz)
    force = forcing.reshape(comps, steps, rows, nz)
    kinds = inverse_bank.shape[0]
    size_t = lax.axis_size("tm")
    coarse = steps * size_t // FACTOR
    half = size_t // 2
    share = rows // size_t

    (tail,) = call(
        tail_kernel,
        [shape_of(comps, 2, rows, nz)],
        [guess, force],
        specs=[
            pl.BlockSpec((comps, 2, rows, nz), lambda i: (0, steps // 2 - 1, 0, 0)),
            pl.BlockSpec((comps, 1, rows, nz), lambda i: (0, steps - 1, 0, 0)),
        ],
        limit=53.5,
        grid=(1,),
    )
    tail = lax.ppermute(tail, "tm", [(i, i + 1) for i in range(size_t - 1)])

    visc, kind_rows, weights = call(
        tables_kernel,
        [shape_of(rows, nz), shape_of(rows, nz), shape_of(64, 64 * kinds, kind=BF16)],
        [visc_table, visc_class, inverse_bank, patch_kind],
        [pltpu.VMEM((rows // 4, nz // 2), F32)],
        [pl.BlockSpec(memory_space=pltpu.SMEM)] + [whole_spec()] * 3,
    )

    last = rows // 8 - 1
    edge = (comps, steps, 8, nz)
    t_edge = (comps, 1, 8, nz)
    length = comps * (steps + 1) * 4 + 8
    first = call(
        first_message_kernel,
        [shape_of(length, nz)] * 2,
        [guess, guess, tail, tail, visc, kind_rows],
        specs=[
            pl.BlockSpec(edge, lambda i: (0, 0, 0, 0)),
            pl.BlockSpec(edge, lambda i: (0, 0, last, 0)),
            pl.BlockSpec(t_edge, lambda i: (0, 0, 0, 0)),
            pl.BlockSpec(t_edge, lambda i: (0, 0, last, 0)),
            whole_spec(),
            whole_spec(),
        ],
        grid=(1,),
    )
    first_in = swapped(first)

    field = shape_of(comps, steps, rows, nz)
    operand = pltpu.VMEM((64 * kinds, (steps + 1) * nz), BF16)
    (inner,) = call(
        first_inner_kernel,
        [shape_of(comps, steps + 1, rows - 2 * TILE, nz)],
        [guess, force, tail, visc, kind_rows, weights],
        [operand],
        flops=10**7,
    )
    length_2 = 8 * comps * steps + 4 * comps * coarse
    done = []
    message = shape_of(length_2, nz)
    for which in range(2):
        done.append(
            call(
                functools.partial(first_side_kernel, which=which, coarse=coarse),
                [shape_of(comps, steps + 1, TILE, nz), message, shape_of(24, nz)] + [message] * which,
                [guess, force, tail, inner, first_in[which], visc, kind_rows, weights]
                + [made[1] for made in done],
                [
                    pltpu.VMEM((comps, steps + 1, 24, nz), F32),
                    pltpu.VMEM((comps, steps, 24, nz), F32),
                    operand,
                ],
                flops=5 * 10**6,
            )
        )
    (straight, _, straight_visc), (diagonal, diagonal_message, diagonal_visc, straight_message) = done
    iterate, visc_loc = (straight, diagonal), (straight_visc, diagonal_visc)
    second = (straight_message, diagonal_message)
    second_in = swapped(second)

    inner_smooth, inner_sums = call(
        second_inner_kernel,
        [shape_of(comps, steps, rows - 2 * TILE, nz), shape_of(rows // TILE - 2, 2, comps, coarse, TILE, nz)],
        [*iterate, inner, force, visc, kind_rows, weights],
        [pltpu.VMEM((comps, steps + 1, rows, nz), F32), operand],
        flops=10**7,
    )
    done = []
    for which in range(2):
        done.append(
            call(
                functools.partial(second_side_kernel, which=which),
                [
                    shape_of(comps, steps, TILE, nz),
                    shape_of(2, comps, coarse, TILE, nz),
                    shape_of(comps, coarse, 4, nz),
                ],
                [iterate[which], inner, force, first_in[which], second_in[which]]
                + [visc_loc[which], kind_rows, weights, done[0][2] if which else visc],
                [
                    pltpu.VMEM((comps, steps, 24, nz), F32),
                    pltpu.VMEM((64 * kinds, max(steps, 2 * coarse) * nz), BF16),
                ],
                flops=5 * 10**6,
            )
        )
    smooth, sums, halo = zip(*done)
    piece = (comps, coarse, share, nz)
    keep, give = call(
        parts_kernel,
        [shape_of(half, *piece)] * 2,
        [*sums, *halo, *visc_loc, inner_sums, visc],
        [
            pltpu.VMEM((comps, coarse, rows + 16, nz), F32),
            pltpu.VMEM((comps, coarse, rows, nz), F32),
            pltpu.VMEM((rows + 16, nz), F32),
            pltpu.VMEM((size_t, *piece), F32),
        ],
    )
    given = lax.ppermute(give, "tm", [(i, i ^ 1) for i in range(size_t)])
    (smoothed,) = call(join_kernel, [field], [*smooth, inner_smooth])
    far_first = list(range(half - 1, 0, -1))
    far_first[:2] = far_first[1::-1]
    *others, own = call(
        functools.partial(pair_kernel, order=far_first + [0]),
        [shape_of(*piece)] * half,
        [keep, given],
        [pltpu.VMEM((half, *piece), F32)],
    )
    arrived = [
        lax.ppermute(other, "tm", [(i, i ^ (2 * d)) for i in range(size_t)])
        for d, other in zip(far_first, others)
    ]
    (result,) = call(total_kernel, [shape_of(comps, coarse, share * nz)], [*arrived, own])
    return (smoothed.reshape(initial_guess.shape), result)


def solution(mesh):
    return jax.shard_map(
        per_device,
        mesh=mesh,
        in_specs=(
            P(None, "tm", "space", None, None),
            P(None, "tm", "space", None, None),
            P(),
            P("space", None, None),
            P(),
            P("space", None, None),
        ),
        out_specs=(P(None, "tm", "space", None, None), P(None, None, ("space", "tm"))),
        check_vma=False,
    )
```

time: 124 us -> 36.6 us (0.30)
  the two profiles are of different devices: /device:TPU:0 before, /device:TPU:4 now
where the time goes in v1:
time: 36.6 us; the launch traced here: 36.4 us
  starting transfers between devices  14.6 us (40%)
  waiting for transfers between devices  13.2 us (36%)
  Pallas kernels  7.69 us (21%)
  between operations  0.83 us (2%)
    ppermute x4, waiting for transfers between devices, swapped(): lax.ppermute(message, 'space', pairs + [(j, i) for i, j in pairs])  9.17 us
    pallas_call x13, Pallas kernels, call(): pl.pallas_call(kernel, out_shape=outs, in_specs=specs or [whole_spec()] *...  7.69 us
    ppermute x3, starting transfers between devices, per_device(): lax.ppermute(other, 'tm', [(i, i ^ 2 * d) for i in range(size_t)])  6.57 us
    ppermute x4, starting transfers between devices, swapped(): lax.ppermute(message, 'space', pairs + [(j, i) for i, j in pairs])  6.12 us
    ppermute x3, waiting for transfers between devices, per_device(): lax.ppermute(other, 'tm', [(i, i ^ 2 * d) for i in range(size_t)])  2.91 us
    ppermute x1, starting transfers between devices, per_device(): tail = lax.ppermute(tail, 'tm', [(i, i + 1) for i in range(size_t - 1)])  1.75 us
    ppermute x1, waiting for transfers between devices, per_device(): given = lax.ppermute(give, 'tm', [(i, i ^ 1) for i in range(size_t)])  1.14 us
  transfers between devices with their start and end apart: 9, of which 6 were waited for; matrix products, arithmetic and copies ran while one was open for 0% of the time, Pallas kernels for 13%

profile of v1, /device:TPU:4, one launch (start us, length us, event | category | flops | bytes accessed | tf_op | source)
XLA Modules:
  0.0 36.4 jit_solution(162590353191812788)
XLA Ops:
  0.6 0.0 copy-start.2
  0.6 0.0 copy-start.3
  0.7 0.0 copy-start.4
  0.7 0.0 copy-start.5
  0.7 0.0 copy-start.1
  0.7 1.0 %shard_map.77 = f32[4,2,32,128]{3,2,1,0:T(8,128)S(1)} custom-call(f32[4,8,32,128]{3,2,1,0:T(8,128)} %bitcast.10, f32[4,8,32,128]{3,2,1,0:T(8,128)} %bitcast.3), custom_call_target="tpu_custom_call" | custom-call | flops 1000000 | bytes 1179648 | tf_op jit(solution)/shard_map/pallas_call | solution.py:607
  1.7 1.7 %collective-permute-start = (f32[4,2,32,128]{3,2,1,0:T(8,128)S(1)}, f32[4,2,32,128]{3,2,1,0:T(8,128)S(1)}, u32[]{:S(2)}, u32[]{:S(2)}) collective-permute-start(f32[4,2,32,128]{3,2,1,0:T(8,128)S(1)} %shard_map.77), channel_id=1, source_target_pairs={{0,1},{1,2},{2,3},{3,4},{4,5},{5,6},{6,7},{8,9},{9,10},{10,11},{11... | collective-permute-start | bytes 393224 | tf_op jit(solution)/shard_map/ppermute | solution.py:654
  3.4 0.0 copy-done.2
  3.4 0.0 copy-done.3
  3.4 0.0 copy-done.4
  3.5 0.0 copy-done.5
  3.5 1.0 %shard_map.78 = (f32[32,128]{1,0:T(8,128)S(1)}, f32[32,128]{1,0:T(8,128)S(1)}, bf16[64,256]{1,0:T(8,128)(2,1)S(1)}) custom-call(f32[8]{0:T(128)S(1)} %copy-done.5, s32[8,4,128]{2,1,0:T(4,128)S(1)} %copy-done.3, bf16[4,32,32]{2,1,0:T(8,128)(2,1)S(1)} %copy-done.2, s32[4,2,64]{2,1,0:T(2,128)S(1)} %copy-done.4), custom_call_target="tpu_custom_call" | custom-call | flops 1000000 | bytes 92192 | tf_op jit(solution)/shard_map/pallas_call | solution.py:607
  4.5 0.0 collective-permute-done.t_ref.t_low_ref.t_high_ref
  4.5 0.0 copy-done.1
  4.5 0.0 copy-start
  4.5 0.1 shard_map.80
  4.6 1.6 %collective-permute-start.1 = (f32[152,128]{1,0:T(8,128)S(1)}, f32[152,128]{1,0:T(8,128)S(1)}, u32[]{:S(2)}, u32[]{:S(2)}) collective-permute-start(f32[152,128]{1,0:T(8,128)S(1)} %get-tuple-element.31), channel_id=1, source_target_pairs={{0,8},{16,24},{8,0},{24,16},{1,9},{17,25},{9,1},{25,17},{2,10},{18... | collective-permute-start | bytes 233480 | tf_op jit(solution)/shard_map/ppermute | solution.py:624
  6.1 1.9 %collective-permute-start.2 = (f32[152,128]{1,0:T(8,128)S(1)}, f32[152,128]{1,0:T(8,128)S(1)}, u32[]{:S(2)}, u32[]{:S(2)}) collective-permute-start(f32[152,128]{1,0:T(8,128)S(1)} %get-tuple-element.33), channel_id=1, source_target_pairs={{8,16},{16,8},{9,17},{17,9},{10,18},{18,10},{11,19},{19,11},{12,20... | collective-permute-start | bytes 233480 | tf_op jit(solution)/shard_map/ppermute | solution.py:624
  8.1 0.0 copy-done
  8.1 0.7 %shard_map.79.inner_ref = f32[4,9,16,128]{3,2,1,0:T(8,128)S(1)} custom-call(f32[4,8,32,128]{3,2,1,0:T(8,128)S(1)} %bitcast.13, f32[4,8,32,128]{3,2,1,0:T(8,128)S(1)} %bitcast.4, f32[4,2,32,128]{3,2,1,0:T(8,128)S(1)} %collective-permute-done.t_ref.t_low_ref.t_high_ref, f32[32,128]{1,0:T(8,128)S(1)} %get-tuple-element.28.visc_ref.after_ref, ...), custom_call_target="tpu_custom_call" | custom-call | flops 10000000 | bytes 1540096 | tf_op jit(solution)/shard_map/pallas_call | solution.py:607
  8.8 0.3 collective-permute-done.1.in_ref.first_ref
  9.1 0.6 %shard_map.81 = (f32[4,9,8,128]{3,2,1,0:T(8,128)S(1)}, f32[288,128]{1,0:T(8,128)S(1)}, f32[24,128]{1,0:T(8,128)S(1)}) custom-call(f32[4,8,32,128]{3,2,1,0:T(8,128)S(1)} %bitcast.14, f32[4,8,32,128]{3,2,1,0:T(8,128)S(1)} %bitcast.5, f32[4,2,32,128]{3,2,1,0:T(8,128)S(1)} %collective-permute-done.t_ref.t_low_ref.t_high_ref, ...), custom_call_target="tpu_custom_call" | custom-call | flops 5000000 | bytes 1925120 | tf_op jit(solution)/shard_map/pallas_call | solution.py:607
  9.7 3.7 %collective-permute-done.2.in_ref.first_ref = f32[152,128]{1,0:T(8,128)S(1)} collective-permute-done((f32[152,128]{1,0:T(8,128)S(1)}, f32[152,128]{1,0:T(8,128)S(1)}, u32[]{:S(2)}, u32[]{:S(2)}) %collective-permute-start.2) | collective-permute-done | bytes 77856 | tf_op jit(solution)/shard_map/ppermute | solution.py:624
  13.3 0.6 %shard_map.82 = (f32[4,9,8,128]{3,2,1,0:T(8,128)S(1)}, f32[288,128]{1,0:T(8,128)S(1)}, f32[24,128]{1,0:T(8,128)S(1)}, f32[288,128]{1,0:T(8,128)S(1)}) custom-call(f32[4,8,32,128]{3,2,1,0:T(8,128)S(1)} %bitcast.15, f32[4,8,32,128]{3,2,1,0:T(8,128)S(1)} %bitcast.6, f32[4,2,32,128]{3,2,1,0:T(8,128)S(1)} %collective-permute-done.t_ref.t_low_ref.t_high_ref, ...), custom_call_target="tpu_custom_call" | custom-call | flops 5000000 | bytes 2220032 | tf_op jit(solution)/shard_map/pallas_call | solution.py:607
  14.0 0.1 collective-permute-start.3
  14.1 2.6 %collective-permute-start.4 = (f32[288,128]{1,0:T(8,128)S(1)}, f32[288,128]{1,0:T(8,128)S(1)}, u32[]{:S(2)}, u32[]{:S(2)}) collective-permute-start(f32[288,128]{1,0:T(8,128)S(1)} %get-tuple-element.39), channel_id=1, source_target_pairs={{8,16},{16,8},{9,17},{17,9},{10,18},{18,10},{11,19},{19,11},{12,20... | collective-permute-start | bytes 442376 | tf_op jit(solution)/shard_map/ppermute | solution.py:624
  16.6 0.8 %shard_map.85 = (f32[4,8,16,128]{3,2,1,0:T(8,128)S(1)}, f32[2,2,4,2,8,128]{5,4,3,2,1,0:T(8,128)S(1)}) custom-call(f32[4,9,8,128]{3,2,1,0:T(8,128)S(1)} %get-tuple-element.32.it_ref.a_ref, f32[4,9,8,128]{3,2,1,0:T(8,128)S(1)} %get-tuple-element.38.it_ref.b_ref, f32[4,9,16,128]{3,2,1,0:T(8,128)S(1)} %shard_map.79.inner_ref, f32[4,8,32,128]{3,2,1,0:T(8,128)S(1)} %bitcast.7, ...), custom_call_target="tpu_custom_call" | custom-call | flops 10000000 | bytes 1572864 | tf_op jit(solution)/shard_map/pallas_call | solution.py:607
  17.5 3.0 %collective-permute-done.3.in_ref = f32[288,128]{1,0:T(8,128)S(1)} collective-permute-done((f32[288,128]{1,0:T(8,128)S(1)}, f32[288,128]{1,0:T(8,128)S(1)}, u32[]{:S(2)}, u32[]{:S(2)}) %collective-permute-start.3) | collective-permute-done | bytes 147488 | tf_op jit(solution)/shard_map/ppermute | solution.py:624
  20.5 0.6 %shard_map.83 = (f32[4,8,8,128]{3,2,1,0:T(8,128)S(1)}, f32[2,4,2,8,128]{4,3,2,1,0:T(8,128)S(1)}, f32[4,2,4,128]{3,2,1,0:T(4,128)S(1)}) custom-call(f32[4,9,8,128]{3,2,1,0:T(8,128)S(1)} %get-tuple-element.32.it_ref.a_ref, f32[4,9,16,128]{3,2,1,0:T(8,128)S(1)} %shard_map.79.inner_ref, f32[4,8,32,128]{3,2,1,0:T(8,128)S(1)} %bitcast.8, ...), custom_call_target="tpu_custom_call" | custom-call | flops 5000000 | bytes 1482752 | tf_op jit(solution)/shard_map/pallas_call | solution.py:607
  21.1 2.2 %collective-permute-done.4.in_ref = f32[288,128]{1,0:T(8,128)S(1)} collective-permute-done((f32[288,128]{1,0:T(8,128)S(1)}, f32[288,128]{1,0:T(8,128)S(1)}, u32[]{:S(2)}, u32[]{:S(2)}) %collective-permute-start.4) | collective-permute-done | bytes 147488 | tf_op jit(solution)/shard_map/ppermute | solution.py:624
  23.3 0.6 %shard_map.84 = (f32[4,8,8,128]{3,2,1,0:T(8,128)S(1)}, f32[2,4,2,8,128]{4,3,2,1,0:T(8,128)S(1)}, f32[4,2,4,128]{3,2,1,0:T(4,128)S(1)}) custom-call(f32[4,9,8,128]{3,2,1,0:T(8,128)S(1)} %get-tuple-element.38.it_ref.b_ref, f32[4,9,16,128]{3,2,1,0:T(8,128)S(1)} %shard_map.79.inner_ref, f32[4,8,32,128]{3,2,1,0:T(8,128)S(1)} %bitcast.9, ...), custom_call_target="tpu_custom_call" | custom-call | flops 5000000 | bytes 1482752 | tf_op jit(solution)/shard_map/pallas_call | solution.py:607
  23.9 0.2 shard_map.87
  24.1 0.2 collective-permute-start.5
  24.3 1.1 %collective-permute-done.5.given_ref = f32[4,4,2,4,128]{4,3,2,1,0:T(4,128)S(1)} collective-permute-done((f32[4,4,2,4,128]{4,3,2,1,0:T(4,128)S(1)}, f32[4,4,2,4,128]{4,3,2,1,0:T(4,128)S(1)}, u32[]{:S(2)}, u32[]{:S(2)}) %collective-permute-start.5) | collective-permute-done | bytes 65568 | tf_op jit(solution)/shard_map/ppermute | solution.py:755
  25.4 4.8 %collective-permute-start.6 = (f32[4,2,4,128]{3,2,1,0:T(4,128)S(1)}, f32[4,2,4,128]{3,2,1,0:T(4,128)S(1)}, u32[]{:S(2)}, u32[]{:S(2)}) collective-permute-start(f32[4,2,4,128]{3,2,1,0:T(4,128)S(1)} %get-tuple-element.50), channel_id=1, source_target_pairs={{0,4},{1,5},{2,6},{3,7},{4,0},{5,1},{6,2},{7,3},{8,12},{9,13},{10,... | collective-permute-start | bytes 49160 | tf_op jit(solution)/shard_map/ppermute | solution.py:766
  30.2 1.3 %collective-permute-start.7 = (f32[4,2,4,128]{3,2,1,0:T(4,128)S(1)}, f32[4,2,4,128]{3,2,1,0:T(4,128)S(1)}, u32[]{:S(2)}, u32[]{:S(2)}) collective-permute-start(f32[4,2,4,128]{3,2,1,0:T(4,128)S(1)} %get-tuple-element.51), channel_id=1, source_target_pairs={{0,6},{1,7},{2,4},{3,5},{4,2},{5,3},{6,0},{7,1},{8,14},{9,15},{10,... | collective-permute-start | bytes 49160 | tf_op jit(solution)/shard_map/ppermute | solution.py:766
  31.6 0.4 %collective-permute-start.8 = (f32[4,2,4,128]{3,2,1,0:T(4,128)S(1)}, f32[4,2,4,128]{3,2,1,0:T(4,128)S(1)}, u32[]{:S(2)}, u32[]{:S(2)}) collective-permute-start(f32[4,2,4,128]{3,2,1,0:T(4,128)S(1)} %get-tuple-element.52), channel_id=1, source_target_pairs={{0,2},{1,3},{2,0},{3,1},{4,6},{5,7},{6,4},{7,5},{8,10},{9,11},{10,... | collective-permute-start | bytes 49160 | tf_op jit(solution)/shard_map/ppermute | solution.py:766
  32.0 0.8 %shard_map.86 = f32[4,8,32,128]{3,2,1,0:T(8,128)} custom-call(f32[4,8,8,128]{3,2,1,0:T(8,128)S(1)} %get-tuple-element.37.a_ref, f32[4,8,8,128]{3,2,1,0:T(8,128)S(1)} %get-tuple-element.42.b_ref, f32[4,8,16,128]{3,2,1,0:T(8,128)S(1)} %get-tuple-element.43.inner_ref), custom_call_target="tpu_custom_call" | custom-call | flops 1000000 | bytes 1048576 | tf_op jit(solution)/shard_map/pallas_call | solution.py:607
  32.9 0.0 collective-permute-done.6.refs_0_
  32.9 2.9 %collective-permute-done.7.refs_1_ = f32[4,2,4,128]{3,2,1,0:T(4,128)S(1)} collective-permute-done((f32[4,2,4,128]{3,2,1,0:T(4,128)S(1)}, f32[4,2,4,128]{3,2,1,0:T(4,128)S(1)}, u32[]{:S(2)}, u32[]{:S(2)}) %collective-permute-start.7) | collective-permute-done | bytes 16416 | tf_op jit(solution)/shard_map/ppermute | solution.py:766
  35.8 0.0 collective-permute-done.8.refs_2_
  35.8 0.6 %shard_map.89 = f32[4,2,512]{2,1,0:T(2,128)} custom-call(f32[4,2,4,128]{3,2,1,0:T(4,128)S(1)} %collective-permute-done.6.refs_0_, f32[4,2,4,128]{3,2,1,0:T(4,128)S(1)} %collective-permute-done.7.refs_1_, f32[4,2,4,128]{3,2,1,0:T(4,128)S(1)} %collective-permute-done.8.refs_2_, f32[4,2,4,128]{3,2,1,0:T(4,128)S(1)} %get-tuple-element.53.refs_3_), custom_call_target="tpu_custom_call" | custom-call | flops 1000000 | bytes 81920 | tf_op jit(solution)/shard_map/pallas_call | solution.py:607
  (1 shorter events, 0.0 us)
Async XLA Ops:
  0.6 2.8 %copy-start.2 = (bf16[4,32,32]{2,1,0:T(8,128)(2,1)S(1)}, bf16[4,32,32]{2,1,0:T(8,128)(2,1)}, u32[]{:S(2)}) copy-start(bf16[4,32,32]{2,1,0:T(8,128)(2,1)} %bank_ref.1) | copy-start | bytes 24580
  0.6 2.8 %copy-start.3 = (s32[8,4,128]{2,1,0:T(4,128)S(1)}, s32[8,4,128]{2,1,0:T(4,128)}, u32[]{:S(2)}) copy-start(s32[8,4,128]{2,1,0:T(4,128)} %class_ref.1) | copy-start | bytes 49156
  0.7 2.8 %copy-start.4 = (s32[4,2,64]{2,1,0:T(2,128)S(1)}, s32[4,2,64]{2,1,0:T(2,128)}, u32[]{:S(2)}) copy-start(s32[4,2,64]{2,1,0:T(2,128)} %kind_ref.1) | copy-start | bytes 6148
  0.7 2.8 %copy-start.5 = (f32[8]{0:T(128)S(1)}, f32[8]{0:T(128)}, u32[]{:S(2)}) copy-start(f32[8]{0:T(128)} %table_ref.1) | copy-start | bytes 100
  0.7 3.8 %copy-start.1 = (f32[4,8,8,4,128]{4,3,2,1,0:T(4,128)S(1)}, f32[4,8,8,4,128]{4,3,2,1,0:T(4,128)}, u32[]{:S(2)}) copy-start(f32[4,8,8,4,128]{4,3,2,1,0:T(4,128)} %param.6) | copy-start | bytes 1572868
  1.7 2.8 %collective-permute-start = (f32[4,2,32,128]{3,2,1,0:T(8,128)S(1)}, f32[4,2,32,128]{3,2,1,0:T(8,128)S(1)}, u32[]{:S(2)}, u32[]{:S(2)}) collective-permute-start(f32[4,2,32,128]{3,2,1,0:T(8,128)S(1)} %shard_map.77), channel_id=1, source_target_pairs={{0,1},{1,2},{2,3},{3,4},{4,5},{5,6},{6,7},{8,9},{9,10},{10,11},{11... | collective-permute-start | bytes 393224 | tf_op jit(solution)/shard_map/ppermute | solution.py:654
  4.5 3.6 %copy-start = (f32[4,8,8,4,128]{4,3,2,1,0:T(4,128)S(1)}, f32[4,8,8,4,128]{4,3,2,1,0:T(4,128)}, u32[]{:S(2)}) copy-start(f32[4,8,8,4,128]{4,3,2,1,0:T(4,128)} %param.7) | copy-start | bytes 1572868
  4.6 4.5 %collective-permute-start.1 = (f32[152,128]{1,0:T(8,128)S(1)}, f32[152,128]{1,0:T(8,128)S(1)}, u32[]{:S(2)}, u32[]{:S(2)}) collective-permute-start(f32[152,128]{1,0:T(8,128)S(1)} %get-tuple-element.31), channel_id=1, source_target_pairs={{0,8},{16,24},{8,0},{24,16},{1,9},{17,25},{9,1},{25,17},{2,10},{18... | collective-permute-start | bytes 233480 | tf_op jit(solution)/shard_map/ppermute | solution.py:624
  6.1 7.2 %collective-permute-start.2 = (f32[152,128]{1,0:T(8,128)S(1)}, f32[152,128]{1,0:T(8,128)S(1)}, u32[]{:S(2)}, u32[]{:S(2)}) collective-permute-start(f32[152,128]{1,0:T(8,128)S(1)} %get-tuple-element.33), channel_id=1, source_target_pairs={{8,16},{16,8},{9,17},{17,9},{10,18},{18,10},{11,19},{19,11},{12,20... | collective-permute-start | bytes 233480 | tf_op jit(solution)/shard_map/ppermute | solution.py:624
  14.0 6.5 %collective-permute-start.3 = (f32[288,128]{1,0:T(8,128)S(1)}, f32[288,128]{1,0:T(8,128)S(1)}, u32[]{:S(2)}, u32[]{:S(2)}) collective-permute-start(f32[288,128]{1,0:T(8,128)S(1)} %get-tuple-element.35), channel_id=1, source_target_pairs={{0,8},{16,24},{8,0},{24,16},{1,9},{17,25},{9,1},{25,17},{2,10},{18... | collective-permute-start | bytes 442376 | tf_op jit(solution)/shard_map/ppermute | solution.py:624
  14.1 9.2 %collective-permute-start.4 = (f32[288,128]{1,0:T(8,128)S(1)}, f32[288,128]{1,0:T(8,128)S(1)}, u32[]{:S(2)}, u32[]{:S(2)}) collective-permute-start(f32[288,128]{1,0:T(8,128)S(1)} %get-tuple-element.39), channel_id=1, source_target_pairs={{8,16},{16,8},{9,17},{17,9},{10,18},{18,10},{11,19},{19,11},{12,20... | collective-permute-start | bytes 442376 | tf_op jit(solution)/shard_map/ppermute | solution.py:624
  24.1 1.3 %collective-permute-start.5 = (f32[4,4,2,4,128]{4,3,2,1,0:T(4,128)S(1)}, f32[4,4,2,4,128]{4,3,2,1,0:T(4,128)S(1)}, u32[]{:S(2)}, u32[]{:S(2)}) collective-permute-start(f32[4,4,2,4,128]{4,3,2,1,0:T(4,128)S(1)} %get-tuple-element.49), channel_id=1, source_target_pairs={{0,1},{1,0},{2,3},{3,2},{4,5},{5,4},{6,7},{7,6},{8,9},{9,8},{10,11... | collective-permute-start | bytes 196616 | tf_op jit(solution)/shard_map/ppermute | solution.py:755
  25.4 7.4 %collective-permute-start.6 = (f32[4,2,4,128]{3,2,1,0:T(4,128)S(1)}, f32[4,2,4,128]{3,2,1,0:T(4,128)S(1)}, u32[]{:S(2)}, u32[]{:S(2)}) collective-permute-start(f32[4,2,4,128]{3,2,1,0:T(4,128)S(1)} %get-tuple-element.50), channel_id=1, source_target_pairs={{0,4},{1,5},{2,6},{3,7},{4,0},{5,1},{6,2},{7,3},{8,12},{9,13},{10,... | collective-permute-start | bytes 49160 | tf_op jit(solution)/shard_map/ppermute | solution.py:766
  30.2 5.5 %collective-permute-start.7 = (f32[4,2,4,128]{3,2,1,0:T(4,128)S(1)}, f32[4,2,4,128]{3,2,1,0:T(4,128)S(1)}, u32[]{:S(2)}, u32[]{:S(2)}) collective-permute-start(f32[4,2,4,128]{3,2,1,0:T(4,128)S(1)} %get-tuple-element.51), channel_id=1, source_target_pairs={{0,6},{1,7},{2,4},{3,5},{4,2},{5,3},{6,0},{7,1},{8,14},{9,15},{10,... | collective-permute-start | bytes 49160 | tf_op jit(solution)/shard_map/ppermute | solution.py:766
  31.6 4.2 %collective-permute-start.8 = (f32[4,2,4,128]{3,2,1,0:T(4,128)S(1)}, f32[4,2,4,128]{3,2,1,0:T(4,128)S(1)}, u32[]{:S(2)}, u32[]{:S(2)}) collective-permute-start(f32[4,2,4,128]{3,2,1,0:T(4,128)S(1)} %get-tuple-element.52), channel_id=1, source_target_pairs={{0,2},{1,3},{2,0},{3,1},{4,6},{5,7},{6,4},{7,5},{8,10},{9,11},{10,... | collective-permute-start | bytes 49160 | tf_op jit(solution)/shard_map/ppermute | solution.py:766

commit v2 on v1

--- a/solution.py
+++ b/solution.py
@@ -288,10 +288,9 @@
     coarse,
 ):
     if which:
-        straight_ref, it_ref, out_ref, visc_loc, passed_ref, u_ref, v_ref, x_ref = refs
-        passed_ref[...] = straight_ref[...]
+        _, it_ref, out_ref, visc_loc, u_ref, v_ref, x_ref = refs
     else:
-        it_ref, out_ref, visc_loc, u_ref, v_ref, x_ref = refs
+        it_ref, out_ref, visc_loc, u_ref, x_ref = refs
     steps, rows = guess_ref.shape[1], guess_ref.shape[2]
     start = lax.axis_index("tm") * steps
     masks = edge_masks()
@@ -328,13 +327,20 @@
             g, 8 - TILE * g, ats, guess, guess_ref, forcing_ref, t_ref, coefs, masks, kinds_ref, w_ref, x_ref, put
         )
 
+        edge, inner = (0, 4) if side == 0 else (4, 0)
+        for c in range(4):
+            for n in range(steps):
+                at = (c * steps + n) * 4
+                out_ref[at : at + 4] = it_ref[c, n + 1, edge : edge + 4]
+        if not which:
+            return
+
         v_ref[:, :, halo] = jnp.zeros((4, steps, 4, 128), F32)
         v_ref[:, :, 8:16] = it_ref[:, 1:]
         if side == 0:
             v_ref[:, :, 16:20] = inner_ref[:, 1:, 0:4]
         else:
             v_ref[:, :, 4:8] = inner_ref[:, 1:, rows - 2 * TILE - 4 : rows - 2 * TILE]
-        edge, inner = (0, 4) if side == 0 else (4, 0)
         sums = [[None] * coarse for _ in range(4)]
         for n in range(steps):
             force = [forcing_ref[c, n, own] for c in range(4)]
@@ -342,7 +348,6 @@
             tiles = residual(tiles_at(v_ref, n), before, force, 8, coefs, masks)
             for c in range(4):
                 at = (c * steps + n) * 4
-                out_ref[at : at + 4] = v_ref[c, n, 8 + edge : 12 + edge]
                 out_ref[count + at : count + at + 4] = tiles[c][edge : edge + 4]
                 rounded = tiles[c].astype(BF16).astype(F32)
                 for k in range(coarse):
@@ -449,22 +454,7 @@
     masks = edge_masks()
     weights = block_weights(steps, coarse)
 
-    def work(side):
-        g = 0 if side == 0 else rows // TILE - 1
-        if side == 0:
-            inside, outer, edge, sign = 8, 4, 4, 1.0
-            exists = space > 0
-            v_ref[:, :, 16:20] = inner_ref[:, 1:, 0:4]
-        else:
-            inside, outer, edge, sign = 12, 16, 0, -1.0
-            exists = space < lax.axis_size("space") - 1
-            v_ref[:, :, 4:8] = inner_ref[:, 1:, rows - 2 * TILE - 4 : rows - 2 * TILE]
-        v_ref[:, :, 8:16] = it_ref[:, 1:]
-        for c in range(4):
-            for n in range(steps):
-                at = (c * steps + n) * 4
-                v_ref[c, n, outer : outer + 4] = in_ref[at : at + 4]
-
+    def beside(side, inside, outer, edge, sign, exists):
         kappa = 0.5 * (visc_loc[inside : inside + 4] + visc_loc[outer : outer + 4])
         sums = [[None] * coarse for _ in range(4)]
         plain = [[None] * coarse for _ in range(4)]
@@ -481,8 +471,8 @@
                     one, two = weights[k][n] * rounded, weights[k][n] * value
                     sums[c][k] = one if n == 0 else sums[c][k] + one
                     plain[c][k] = two if n == 0 else plain[c][k] + two
-        beside = first_ref[static + 4 : static + 8]
-        chosen = kind_masks(jnp.concatenate([beside] * 2, axis=0), kinds)
+        kind_rows = first_ref[static + 4 : static + 8]
+        chosen = kind_masks(jnp.concatenate([kind_rows] * 2, axis=0), kinds)
         for k in range(coarse):
             tiles = []
             for c in range(4):
@@ -501,6 +491,24 @@
                 change = (one[c] + two[c])[edge : edge + 4]
                 halo_ref[c, k] = exists * (plain[c][k] + change)
 
+    def work(side):
+        g = 0 if side == 0 else rows // TILE - 1
+        if side == 0:
+            inside, outer, edge, sign = 8, 4, 4, 1.0
+            exists = space > 0
+            v_ref[:, :, 16:20] = inner_ref[:, 1:, 0:4]
+        else:
+            inside, outer, edge, sign = 12, 16, 0, -1.0
+            exists = space < lax.axis_size("space") - 1
+            v_ref[:, :, 4:8] = inner_ref[:, 1:, rows - 2 * TILE - 4 : rows - 2 * TILE]
+        v_ref[:, :, 8:16] = it_ref[:, 1:]
+        for c in range(4):
+            for n in range(steps):
+                at = (c * steps + n) * 4
+                v_ref[c, n, outer : outer + 4] = in_ref[at : at + 4]
+
+        if which:
+            beside(side, inside, outer, edge, sign, exists)
         totals = Restriction(weights, forcing_ref, smooth_ref, -TILE * g)
         coefs = coefficients(visc_loc, 8, masks)
         second_sweep(
@@ -510,6 +518,8 @@
             for k in range(coarse):
                 sums_ref[0, c, k] = totals.held[c][k]
                 sums_ref[1, c, k] = totals.rest[c][k]
+                if not which:
+                    halo_ref[c, k] = totals.held[c][k][4 - edge : 8 - edge]
 
     by_side(which, work)
 
@@ -692,25 +702,21 @@
     )
     length_2 = 8 * comps * steps + 4 * comps * coarse
     done = []
-    message = shape_of(length_2, nz)
+    messages = [shape_of(4 * comps * steps, nz), shape_of(length_2, nz)]
     for which in range(2):
         done.append(
             call(
                 functools.partial(first_side_kernel, which=which, coarse=coarse),
-                [shape_of(comps, steps + 1, TILE, nz), message, shape_of(24, nz)] + [message] * which,
+                [shape_of(comps, steps + 1, TILE, nz), messages[which], shape_of(24, nz)],
                 [guess, force, tail, inner, first_in[which], visc, kind_rows, weights]
-                + [made[1] for made in done],
-                [
-                    pltpu.VMEM((comps, steps + 1, 24, nz), F32),
-                    pltpu.VMEM((comps, steps, 24, nz), F32),
-                    operand,
-                ],
+                + [made[2] for made in done],
+                [pltpu.VMEM((comps, steps + 1, 24, nz), F32)]
+                + [pltpu.VMEM((comps, steps, 24, nz), F32)] * which
+                + [operand],
                 flops=5 * 10**6,
             )
         )
-    (straight, _, straight_visc), (diagonal, diagonal_message, diagonal_visc, straight_message) = done
-    iterate, visc_loc = (straight, diagonal), (straight_visc, diagonal_visc)
-    second = (straight_message, diagonal_message)
+    iterate, second, visc_loc = zip(*done)
     second_in = swapped(second)
 
     inner_smooth, inner_sums = call(
@@ -718,7 +724,7 @@
         [shape_of(comps, steps, rows - 2 * TILE, nz), shape_of(rows // TILE - 2, 2, comps, coarse, TILE, nz)],
         [*iterate, inner, force, visc, kind_rows, weights],
         [pltpu.VMEM((comps, steps + 1, rows, nz), F32), operand],
-        flops=10**7,
+        flops=10**10,
     )
     done = []
     for which in range(2):
@@ -739,12 +745,13 @@
                 flops=5 * 10**6,
             )
         )
-    smooth, sums, halo = zip(*done)
+    smooth, sums, (face, halo) = zip(*done)
+    (face,) = swapped([face])
     piece = (comps, coarse, share, nz)
     keep, give = call(
         parts_kernel,
         [shape_of(half, *piece)] * 2,
-        [*sums, *halo, *visc_loc, inner_sums, visc],
+        [*sums, face, halo, *visc_loc, inner_sums, visc],
         [
             pltpu.VMEM((comps, coarse, rows + 16, nz), F32),
             pltpu.VMEM((comps, coarse, rows, nz), F32),

time: 36.6 us -> 37.6 us (1.027)
  the two profiles are of different devices: /device:TPU:4 before, /device:TPU:0 now
where the time goes in v2:
time: 37.6 us; the launch traced here: 37.4 us
  starting transfers between devices  20.4 us (54%)
  waiting for transfers between devices  8.72 us (23%)
  Pallas kernels  7.46 us (20%)
  between operations  0.83 us (2%)
    ppermute x5, starting transfers between devices, swapped(): lax.ppermute(message, 'space', pairs + [(j, i) for i, j in pairs])  10.8 us
    pallas_call x13, Pallas kernels, call(): pl.pallas_call(kernel, out_shape=outs, in_specs=specs or [whole_spec()] *...  7.46 us
    ppermute x3, starting transfers between devices, per_device(): lax.ppermute(other, 'tm', [(i, i ^ 2 * d) for i in range(size_t)])  6.44 us
    ppermute x5, waiting for transfers between devices, swapped(): lax.ppermute(message, 'space', pairs + [(j, i) for i, j in pairs])  4.65 us
    ppermute x3, waiting for transfers between devices, per_device(): lax.ppermute(other, 'tm', [(i, i ^ 2 * d) for i in range(size_t)])  3.16 us
    ppermute x1, starting transfers between devices, per_device(): tail = lax.ppermute(tail, 'tm', [(i, i + 1) for i in range(size_t - 1)])  2.36 us
    ppermute x1, waiting for transfers between devices, per_device(): given = lax.ppermute(give, 'tm', [(i, i ^ 1) for i in range(size_t)])  0.9 us
    ppermute x1, starting transfers between devices, per_device(): given = lax.ppermute(give, 'tm', [(i, i ^ 1) for i in range(size_t)])  0.77 us
  transfers between devices with their start and end apart: 10, of which 5 were waited for; matrix products, arithmetic and copies ran while one was open for 0% of the time, Pallas kernels for 15%

profile of v2, /device:TPU:0, one launch (start us, length us, event | category | flops | bytes accessed | tf_op | source)
XLA Modules:
  0.0 37.4 jit_solution(12967571957834683110)
XLA Ops:
  0.6 0.0 copy-start.2
  0.6 0.0 copy-start.3
  0.7 0.0 copy-start.4
  0.7 0.0 copy-start.5
  0.7 0.0 copy-start
  0.7 1.0 %shard_map.77 = f32[4,2,32,128]{3,2,1,0:T(8,128)S(1)} custom-call(f32[4,8,32,128]{3,2,1,0:T(8,128)} %bitcast.3, f32[4,8,32,128]{3,2,1,0:T(8,128)} %bitcast.9), custom_call_target="tpu_custom_call" | custom-call | flops 1000000 | bytes 1179648 | tf_op jit(solution)/shard_map/pallas_call | solution.py:617
  1.7 2.4 %collective-permute-start = (f32[4,2,32,128]{3,2,1,0:T(8,128)S(1)}, f32[4,2,32,128]{3,2,1,0:T(8,128)S(1)}, u32[]{:S(2)}, u32[]{:S(2)}) collective-permute-start(f32[4,2,32,128]{3,2,1,0:T(8,128)S(1)} %shard_map.77), channel_id=1, source_target_pairs={{0,1},{1,2},{2,3},{3,4},{4,5},{5,6},{6,7},{8,9},{9,10},{10,11},{11... | collective-permute-start | bytes 393224 | tf_op jit(solution)/shard_map/ppermute | solution.py:664
  4.0 0.0 copy-done.2
  4.0 0.0 copy-done.3
  4.1 0.0 copy-done.4
  4.1 0.0 copy-done.5
  4.1 1.0 %shard_map.78 = (f32[32,128]{1,0:T(8,128)S(1)}, f32[32,128]{1,0:T(8,128)S(1)}, bf16[64,256]{1,0:T(8,128)(2,1)S(1)}) custom-call(f32[8]{0:T(128)S(1)} %copy-done.5, s32[8,4,128]{2,1,0:T(4,128)S(1)} %copy-done.3, bf16[4,32,32]{2,1,0:T(8,128)(2,1)S(1)} %copy-done.2, s32[4,2,64]{2,1,0:T(2,128)S(1)} %copy-done.4), custom_call_target="tpu_custom_call" | custom-call | flops 1000000 | bytes 92192 | tf_op jit(solution)/shard_map/pallas_call | solution.py:617
  5.1 0.0 collective-permute-done.t_ref.t_low_ref.t_high_ref
  5.1 0.0 copy-done
  5.1 0.0 copy-start.1
  5.1 0.1 shard_map.80
  5.2 2.4 %collective-permute-start.1 = (f32[152,128]{1,0:T(8,128)S(1)}, f32[152,128]{1,0:T(8,128)S(1)}, u32[]{:S(2)}, u32[]{:S(2)}) collective-permute-start(f32[152,128]{1,0:T(8,128)S(1)} %get-tuple-element.30), channel_id=1, source_target_pairs={{0,8},{16,24},{8,0},{24,16},{1,9},{17,25},{9,1},{25,17},{2,10},{18... | collective-permute-start | bytes 233480 | tf_op jit(solution)/shard_map/ppermute | solution.py:634
  7.6 0.7 %collective-permute-start.3 = (f32[152,128]{1,0:T(8,128)S(1)}, f32[152,128]{1,0:T(8,128)S(1)}, u32[]{:S(2)}, u32[]{:S(2)}) collective-permute-start(f32[152,128]{1,0:T(8,128)S(1)} %get-tuple-element.35), channel_id=1, source_target_pairs={{8,16},{16,8},{9,17},{17,9},{10,18},{18,10},{11,19},{19,11},{12,20... | collective-permute-start | bytes 233480 | tf_op jit(solution)/shard_map/ppermute | solution.py:634
  8.3 0.0 copy-done.1
  8.3 0.7 %shard_map.79.inner_ref = f32[4,9,16,128]{3,2,1,0:T(8,128)S(1)} custom-call(f32[4,8,32,128]{3,2,1,0:T(8,128)S(1)} %bitcast.6, f32[4,8,32,128]{3,2,1,0:T(8,128)S(1)} %bitcast.10, f32[4,2,32,128]{3,2,1,0:T(8,128)S(1)} %collective-permute-done.t_ref.t_low_ref.t_high_ref, f32[32,128]{1,0:T(8,128)S(1)} %get-tuple-element.27.visc_ref.after_ref, ...), custom_call_target="tpu_custom_call" | custom-call | flops 10000000 | bytes 1540096 | tf_op jit(solution)/shard_map/pallas_call | solution.py:617
  9.0 1.0 %collective-permute-done.1.in_ref.first_ref = f32[152,128]{1,0:T(8,128)S(1)} collective-permute-done((f32[152,128]{1,0:T(8,128)S(1)}, f32[152,128]{1,0:T(8,128)S(1)}, u32[]{:S(2)}, u32[]{:S(2)}) %collective-permute-start.1) | collective-permute-done | bytes 77856 | tf_op jit(solution)/shard_map/ppermute | solution.py:634
  10.0 0.5 %shard_map.81 = (f32[4,9,8,128]{3,2,1,0:T(8,128)S(1)}, f32[128,128]{1,0:T(8,128)S(1)}, f32[24,128]{1,0:T(8,128)S(1)}) custom-call(f32[4,8,32,128]{3,2,1,0:T(8,128)S(1)} %bitcast.7, f32[4,8,32,128]{3,2,1,0:T(8,128)S(1)} %bitcast.11, f32[4,2,32,128]{3,2,1,0:T(8,128)S(1)} %collective-permute-done.t_ref.t_low_ref.t_high_ref, ...), custom_call_target="tpu_custom_call" | custom-call | flops 5000000 | bytes 1843200 | tf_op jit(solution)/shard_map/pallas_call | solution.py:617
  10.5 3.3 %collective-permute-start.2 = (f32[128,128]{1,0:T(8,128)S(1)}, f32[128,128]{1,0:T(8,128)S(1)}, u32[]{:S(2)}, u32[]{:S(2)}) collective-permute-start(f32[128,128]{1,0:T(8,128)S(1)} %get-tuple-element.32), channel_id=1, source_target_pairs={{0,8},{16,24},{8,0},{24,16},{1,9},{17,25},{9,1},{25,17},{2,10},{18... | collective-permute-start | bytes 196616 | tf_op jit(solution)/shard_map/ppermute | solution.py:634
  13.8 0.0 collective-permute-done.3.in_ref.first_ref
  13.8 0.6 %shard_map.83 = (f32[4,9,8,128]{3,2,1,0:T(8,128)S(1)}, f32[288,128]{1,0:T(8,128)S(1)}, f32[24,128]{1,0:T(8,128)S(1)}) custom-call(f32[4,8,32,128]{3,2,1,0:T(8,128)S(1)} %bitcast.8, f32[4,8,32,128]{3,2,1,0:T(8,128)S(1)} %bitcast.12, f32[4,2,32,128]{3,2,1,0:T(8,128)S(1)} %collective-permute-done.t_ref.t_low_ref.t_high_ref, ...), custom_call_target="tpu_custom_call" | custom-call | flops 5000000 | bytes 1937408 | tf_op jit(solution)/shard_map/pallas_call | solution.py:617
  14.4 0.7 %collective-permute-start.4 = (f32[288,128]{1,0:T(8,128)S(1)}, f32[288,128]{1,0:T(8,128)S(1)}, u32[]{:S(2)}, u32[]{:S(2)}) collective-permute-start(f32[288,128]{1,0:T(8,128)S(1)} %get-tuple-element.37), channel_id=1, source_target_pairs={{8,16},{16,8},{9,17},{17,9},{10,18},{18,10},{11,19},{19,11},{12,20... | collective-permute-start | bytes 442376 | tf_op jit(solution)/shard_map/ppermute | solution.py:634
  15.1 1.6 %collective-permute-done.2.in_ref = f32[128,128]{1,0:T(8,128)S(1)} collective-permute-done((f32[128,128]{1,0:T(8,128)S(1)}, f32[128,128]{1,0:T(8,128)S(1)}, u32[]{:S(2)}, u32[]{:S(2)}) %collective-permute-start.2) | collective-permute-done | bytes 65568 | tf_op jit(solution)/shard_map/ppermute | solution.py:634
  16.7 0.4 %shard_map.82 = (f32[4,8,8,128]{3,2,1,0:T(8,128)S(1)}, f32[2,4,2,8,128]{4,3,2,1,0:T(8,128)S(1)}, f32[4,2,4,128]{3,2,1,0:T(4,128)S(1)}) custom-call(f32[4,9,8,128]{3,2,1,0:T(8,128)S(1)} %get-tuple-element.31.it_ref.a_ref, f32[4,9,16,128]{3,2,1,0:T(8,128)S(1)} %shard_map.79.inner_ref, f32[4,8,32,128]{3,2,1,0:T(8,128)S(1)} %bitcast.13, ...), custom_call_target="tpu_custom_call" | custom-call | flops 5000000 | bytes 1400832 | tf_op jit(solution)/shard_map/pallas_call | solution.py:617
  17.1 3.7 %collective-permute-start.5 = (f32[4,2,4,128]{3,2,1,0:T(4,128)S(1)}, f32[4,2,4,128]{3,2,1,0:T(4,128)S(1)}, u32[]{:S(2)}, u32[]{:S(2)}) collective-permute-start(f32[4,2,4,128]{3,2,1,0:T(4,128)S(1)} %get-tuple-element.39.after_ref), channel_id=1, source_target_pairs={{0,8},{16,24},{8,0},{24,16},{1,9},{17,25},{9,1},{25,17},{2,10},{18... | collective-permute-start | bytes 49160 | tf_op jit(solution)/shard_map/ppermute | solution.py:634
  20.9 0.8 %shard_map.85 = (f32[4,8,16,128]{3,2,1,0:T(8,128)S(1)}, f32[2,2,4,2,8,128]{5,4,3,2,1,0:T(8,128)S(1)}) custom-call(f32[4,9,8,128]{3,2,1,0:T(8,128)S(1)} %get-tuple-element.31.it_ref.a_ref, f32[4,9,8,128]{3,2,1,0:T(8,128)S(1)} %get-tuple-element.36.it_ref.b_ref, f32[4,9,16,128]{3,2,1,0:T(8,128)S(1)} %shard_map.79.inner_ref, f32[4,8,32,128]{3,2,1,0:T(8,128)S(1)} %bitcast.14, ...), custom_call_target="tpu_custom_call" | custom-call | flops 10000000000 | bytes 1572864 | tf_op jit(solution)/shard_map/pallas_call | solution.py:617
  21.7 0.0 collective-permute-done.4.in_ref
  21.7 0.6 %shard_map.84 = (f32[4,8,8,128]{3,2,1,0:T(8,128)S(1)}, f32[2,4,2,8,128]{4,3,2,1,0:T(8,128)S(1)}, f32[4,2,4,128]{3,2,1,0:T(4,128)S(1)}) custom-call(f32[4,9,8,128]{3,2,1,0:T(8,128)S(1)} %get-tuple-element.36.it_ref.b_ref, f32[4,9,16,128]{3,2,1,0:T(8,128)S(1)} %shard_map.79.inner_ref, f32[4,8,32,128]{3,2,1,0:T(8,128)S(1)} %bitcast.15, ...), custom_call_target="tpu_custom_call" | custom-call | flops 5000000 | bytes 1482752 | tf_op jit(solution)/shard_map/pallas_call | solution.py:617
  22.3 2.1 %collective-permute-done.5.a_halo_ref = f32[4,2,4,128]{3,2,1,0:T(4,128)S(1)} collective-permute-done((f32[4,2,4,128]{3,2,1,0:T(4,128)S(1)}, f32[4,2,4,128]{3,2,1,0:T(4,128)S(1)}, u32[]{:S(2)}, u32[]{:S(2)}) %collective-permute-start.5) | collective-permute-done | bytes 16416 | tf_op jit(solution)/shard_map/ppermute | solution.py:634
  24.4 0.2 shard_map.87
  24.6 0.8 %collective-permute-start.6 = (f32[4,4,2,4,128]{4,3,2,1,0:T(4,128)S(1)}, f32[4,4,2,4,128]{4,3,2,1,0:T(4,128)S(1)}, u32[]{:S(2)}, u32[]{:S(2)}) collective-permute-start(f32[4,4,2,4,128]{4,3,2,1,0:T(4,128)S(1)} %get-tuple-element.47), channel_id=1, source_target_pairs={{0,1},{1,0},{2,3},{3,2},{4,5},{5,4},{6,7},{7,6},{8,9},{9,8},{10,11... | collective-permute-start | bytes 196616 | tf_op jit(solution)/shard_map/ppermute | solution.py:762
  25.4 0.9 %collective-permute-done.6.given_ref = f32[4,4,2,4,128]{4,3,2,1,0:T(4,128)S(1)} collective-permute-done((f32[4,4,2,4,128]{4,3,2,1,0:T(4,128)S(1)}, f32[4,4,2,4,128]{4,3,2,1,0:T(4,128)S(1)}, u32[]{:S(2)}, u32[]{:S(2)}) %collective-permute-start.6) | collective-permute-done | bytes 65568 | tf_op jit(solution)/shard_map/ppermute | solution.py:762
  26.3 4.9 %collective-permute-start.7 = (f32[4,2,4,128]{3,2,1,0:T(4,128)S(1)}, f32[4,2,4,128]{3,2,1,0:T(4,128)S(1)}, u32[]{:S(2)}, u32[]{:S(2)}) collective-permute-start(f32[4,2,4,128]{3,2,1,0:T(4,128)S(1)} %get-tuple-element.48), channel_id=1, source_target_pairs={{0,4},{1,5},{2,6},{3,7},{4,0},{5,1},{6,2},{7,3},{8,12},{9,13},{10,... | collective-permute-start | bytes 49160 | tf_op jit(solution)/shard_map/ppermute | solution.py:773
  31.2 1.3 %collective-permute-start.8 = (f32[4,2,4,128]{3,2,1,0:T(4,128)S(1)}, f32[4,2,4,128]{3,2,1,0:T(4,128)S(1)}, u32[]{:S(2)}, u32[]{:S(2)}) collective-permute-start(f32[4,2,4,128]{3,2,1,0:T(4,128)S(1)} %get-tuple-element.49), channel_id=1, source_target_pairs={{0,6},{1,7},{2,4},{3,5},{4,2},{5,3},{6,0},{7,1},{8,14},{9,15},{10,... | collective-permute-start | bytes 49160 | tf_op jit(solution)/shard_map/ppermute | solution.py:773
  32.6 0.2 collective-permute-start.9
  32.8 0.8 %shard_map.86 = f32[4,8,32,128]{3,2,1,0:T(8,128)} custom-call(f32[4,8,8,128]{3,2,1,0:T(8,128)S(1)} %get-tuple-element.34.a_ref, f32[4,8,8,128]{3,2,1,0:T(8,128)S(1)} %get-tuple-element.40.b_ref, f32[4,8,16,128]{3,2,1,0:T(8,128)S(1)} %get-tuple-element.41.inner_ref), custom_call_target="tpu_custom_call" | custom-call | flops 1000000 | bytes 1048576 | tf_op jit(solution)/shard_map/pallas_call | solution.py:617
  33.6 0.0 collective-permute-done.7.refs_0_
  33.6 3.2 %collective-permute-done.8.refs_1_ = f32[4,2,4,128]{3,2,1,0:T(4,128)S(1)} collective-permute-done((f32[4,2,4,128]{3,2,1,0:T(4,128)S(1)}, f32[4,2,4,128]{3,2,1,0:T(4,128)S(1)}, u32[]{:S(2)}, u32[]{:S(2)}) %collective-permute-start.8) | collective-permute-done | bytes 16416 | tf_op jit(solution)/shard_map/ppermute | solution.py:773
  36.8 0.0 collective-permute-done.9.refs_2_
  36.8 0.6 %shard_map.89 = f32[4,2,512]{2,1,0:T(2,128)} custom-call(f32[4,2,4,128]{3,2,1,0:T(4,128)S(1)} %collective-permute-done.7.refs_0_, f32[4,2,4,128]{3,2,1,0:T(4,128)S(1)} %collective-permute-done.8.refs_1_, f32[4,2,4,128]{3,2,1,0:T(4,128)S(1)} %collective-permute-done.9.refs_2_, f32[4,2,4,128]{3,2,1,0:T(4,128)S(1)} %get-tuple-element.51.refs_3_), custom_call_target="tpu_custom_call" | custom-call | flops 1000000 | bytes 81920 | tf_op jit(solution)/shard_map/pallas_call | solution.py:617
  (1 shorter events, 0.0 us)
Async XLA Ops:
  0.6 3.4 %copy-start.2 = (bf16[4,32,32]{2,1,0:T(8,128)(2,1)S(1)}, bf16[4,32,32]{2,1,0:T(8,128)(2,1)}, u32[]{:S(2)}) copy-start(bf16[4,32,32]{2,1,0:T(8,128)(2,1)} %bank_ref.1) | copy-start | bytes 24580
  0.6 3.4 %copy-start.3 = (s32[8,4,128]{2,1,0:T(4,128)S(1)}, s32[8,4,128]{2,1,0:T(4,128)}, u32[]{:S(2)}) copy-start(s32[8,4,128]{2,1,0:T(4,128)} %class_ref.1) | copy-start | bytes 49156
  0.7 3.4 %copy-start.4 = (s32[4,2,64]{2,1,0:T(2,128)S(1)}, s32[4,2,64]{2,1,0:T(2,128)}, u32[]{:S(2)}) copy-start(s32[4,2,64]{2,1,0:T(2,128)} %kind_ref.1) | copy-start | bytes 6148
  0.7 3.4 %copy-start.5 = (f32[8]{0:T(128)S(1)}, f32[8]{0:T(128)}, u32[]{:S(2)}) copy-start(f32[8]{0:T(128)} %table_ref.1) | copy-start | bytes 100
  0.7 4.4 %copy-start = (f32[4,8,8,4,128]{4,3,2,1,0:T(4,128)S(1)}, f32[4,8,8,4,128]{4,3,2,1,0:T(4,128)}, u32[]{:S(2)}) copy-start(f32[4,8,8,4,128]{4,3,2,1,0:T(4,128)} %param.6) | copy-start | bytes 1572868
  1.7 3.4 %collective-permute-start = (f32[4,2,32,128]{3,2,1,0:T(8,128)S(1)}, f32[4,2,32,128]{3,2,1,0:T(8,128)S(1)}, u32[]{:S(2)}, u32[]{:S(2)}) collective-permute-start(f32[4,2,32,128]{3,2,1,0:T(8,128)S(1)} %shard_map.77), channel_id=1, source_target_pairs={{0,1},{1,2},{2,3},{3,4},{4,5},{5,6},{6,7},{8,9},{9,10},{10,11},{11... | collective-permute-start | bytes 393224 | tf_op jit(solution)/shard_map/ppermute | solution.py:664
  5.1 3.1 %copy-start.1 = (f32[4,8,8,4,128]{4,3,2,1,0:T(4,128)S(1)}, f32[4,8,8,4,128]{4,3,2,1,0:T(4,128)}, u32[]{:S(2)}) copy-start(f32[4,8,8,4,128]{4,3,2,1,0:T(4,128)} %param.7) | copy-start | bytes 1572868
  5.2 4.8 %collective-permute-start.1 = (f32[152,128]{1,0:T(8,128)S(1)}, f32[152,128]{1,0:T(8,128)S(1)}, u32[]{:S(2)}, u32[]{:S(2)}) collective-permute-start(f32[152,128]{1,0:T(8,128)S(1)} %get-tuple-element.30), channel_id=1, source_target_pairs={{0,8},{16,24},{8,0},{24,16},{1,9},{17,25},{9,1},{25,17},{2,10},{18... | collective-permute-start | bytes 233480 | tf_op jit(solution)/shard_map/ppermute | solution.py:634
  7.6 6.2 %collective-permute-start.3 = (f32[152,128]{1,0:T(8,128)S(1)}, f32[152,128]{1,0:T(8,128)S(1)}, u32[]{:S(2)}, u32[]{:S(2)}) collective-permute-start(f32[152,128]{1,0:T(8,128)S(1)} %get-tuple-element.35), channel_id=1, source_target_pairs={{8,16},{16,8},{9,17},{17,9},{10,18},{18,10},{11,19},{19,11},{12,20... | collective-permute-start | bytes 233480 | tf_op jit(solution)/shard_map/ppermute | solution.py:634
  10.5 6.2 %collective-permute-start.2 = (f32[128,128]{1,0:T(8,128)S(1)}, f32[128,128]{1,0:T(8,128)S(1)}, u32[]{:S(2)}, u32[]{:S(2)}) collective-permute-start(f32[128,128]{1,0:T(8,128)S(1)} %get-tuple-element.32), channel_id=1, source_target_pairs={{0,8},{16,24},{8,0},{24,16},{1,9},{17,25},{9,1},{25,17},{2,10},{18... | collective-permute-start | bytes 196616 | tf_op jit(solution)/shard_map/ppermute | solution.py:634
  14.4 7.3 %collective-permute-start.4 = (f32[288,128]{1,0:T(8,128)S(1)}, f32[288,128]{1,0:T(8,128)S(1)}, u32[]{:S(2)}, u32[]{:S(2)}) collective-permute-start(f32[288,128]{1,0:T(8,128)S(1)} %get-tuple-element.37), channel_id=1, source_target_pairs={{8,16},{16,8},{9,17},{17,9},{10,18},{18,10},{11,19},{19,11},{12,20... | collective-permute-start | bytes 442376 | tf_op jit(solution)/shard_map/ppermute | solution.py:634
  17.1 7.3 %collective-permute-start.5 = (f32[4,2,4,128]{3,2,1,0:T(4,128)S(1)}, f32[4,2,4,128]{3,2,1,0:T(4,128)S(1)}, u32[]{:S(2)}, u32[]{:S(2)}) collective-permute-start(f32[4,2,4,128]{3,2,1,0:T(4,128)S(1)} %get-tuple-element.39.after_ref), channel_id=1, source_target_pairs={{0,8},{16,24},{8,0},{24,16},{1,9},{17,25},{9,1},{25,17},{2,10},{18... | collective-permute-start | bytes 49160 | tf_op jit(solution)/shard_map/ppermute | solution.py:634
  24.6 1.7 %collective-permute-start.6 = (f32[4,4,2,4,128]{4,3,2,1,0:T(4,128)S(1)}, f32[4,4,2,4,128]{4,3,2,1,0:T(4,128)S(1)}, u32[]{:S(2)}, u32[]{:S(2)}) collective-permute-start(f32[4,4,2,4,128]{4,3,2,1,0:T(4,128)S(1)} %get-tuple-element.47), channel_id=1, source_target_pairs={{0,1},{1,0},{2,3},{3,2},{4,5},{5,4},{6,7},{7,6},{8,9},{9,8},{10,11... | collective-permute-start | bytes 196616 | tf_op jit(solution)/shard_map/ppermute | solution.py:762
  26.3 7.3 %collective-permute-start.7 = (f32[4,2,4,128]{3,2,1,0:T(4,128)S(1)}, f32[4,2,4,128]{3,2,1,0:T(4,128)S(1)}, u32[]{:S(2)}, u32[]{:S(2)}) collective-permute-start(f32[4,2,4,128]{3,2,1,0:T(4,128)S(1)} %get-tuple-element.48), channel_id=1, source_target_pairs={{0,4},{1,5},{2,6},{3,7},{4,0},{5,1},{6,2},{7,3},{8,12},{9,13},{10,... | collective-permute-start | bytes 49160 | tf_op jit(solution)/shard_map/ppermute | solution.py:773
  31.2 5.5 %collective-permute-start.8 = (f32[4,2,4,128]{3,2,1,0:T(4,128)S(1)}, f32[4,2,4,128]{3,2,1,0:T(4,128)S(1)}, u32[]{:S(2)}, u32[]{:S(2)}) collective-permute-start(f32[4,2,4,128]{3,2,1,0:T(4,128)S(1)} %get-tuple-element.49), channel_id=1, source_target_pairs={{0,6},{1,7},{2,4},{3,5},{4,2},{5,3},{6,0},{7,1},{8,14},{9,15},{10,... | collective-permute-start | bytes 49160 | tf_op jit(solution)/shard_map/ppermute | solution.py:773
  32.6 4.2 %collective-permute-start.9 = (f32[4,2,4,128]{3,2,1,0:T(4,128)S(1)}, f32[4,2,4,128]{3,2,1,0:T(4,128)S(1)}, u32[]{:S(2)}, u32[]{:S(2)}) collective-permute-start(f32[4,2,4,128]{3,2,1,0:T(4,128)S(1)} %get-tuple-element.50), channel_id=1, source_target_pairs={{0,2},{1,3},{2,0},{3,1},{4,6},{5,7},{6,4},{7,5},{8,10},{9,11},{10,... | collective-permute-start | bytes 49160 | tf_op jit(solution)/shard_map/ppermute | solution.py:773
